TPU v7x, 32 devices: a whole 2x2x4 slice. The times are simulated.
32 devices in a mesh: dp: 4 (over z), ctx: 2 (over y), fsdp: 4 (over x, core).
Axes of the slice: x: 2, y: 2, z: 4, core: 2. Of those that a mesh axis runs over, the one named last changes fastest.
Arguments:
- layer_input: bfloat16 [4, 1024, 2560], P('dp', ('ctx', 'fsdp')), may hold values from -6 to 6
- segment_ids: int32 [4, 1024], P('dp'), may hold values from 0 to 3, as said below
- attn_gain: bfloat16 [2560], P('fsdp'), may hold values from 0.099609375 to 1.8984375
- query_down: bfloat16 [2560, 768], P('fsdp'), may hold values from -0.125 to 0.125
- query_gain: bfloat16 [768], P('fsdp'), may hold values from 0.099609375 to 1.8984375
- query_up: bfloat16 [768, 3840], P('fsdp'), may hold values from -0.21875 to 0.21875
- latent_down: bfloat16 [2560, 288], P('fsdp'), may hold values from -0.125 to 0.125
- latent_gain: bfloat16 [256], P('fsdp'), may hold values from 0.099609375 to 1.8984375
- latent_up: bfloat16 [256, 5120], P('fsdp'), may hold values from -0.375 to 0.375
- attn_output: bfloat16 [2560, 2560], P('fsdp'), may hold values from -4 to 4
- ffn_gain: bfloat16 [2560], P('fsdp'), may hold values from 0.099609375 to 1.8984375
- gate_up: bfloat16 [2, 6400, 2560], P(None, 'fsdp'), may hold values from -0.125 to 0.125
- down_proj: bfloat16 [6400, 2560], P('fsdp'), may hold values from -0.75 to 0.75
- cotangent: bfloat16 [4, 1024, 2560], P('dp', ('ctx', 'fsdp')), may hold values from -6 to 6
Outputs:
- layer_output: bfloat16 [4, 1024, 2560], P('dp', ('ctx', 'fsdp'))
- input_grad: float32 [4, 1024, 2560], P('dp', ('ctx', 'fsdp'))
- attn_gain_grad: float32 [2560], P('fsdp')
- query_down_grad: float32 [2560, 768], P('fsdp')
- query_gain_grad: float32 [768], P('fsdp')
- query_up_grad: float32 [768, 3840], P('fsdp')
- latent_down_grad: float32 [2560, 288], P('fsdp')
- latent_gain_grad: float32 [256], P('fsdp')
- latent_up_grad: float32 [256, 5120], P('fsdp')
- attn_output_grad: float32 [2560, 2560], P('fsdp')
- ffn_gain_grad: float32 [2560], P('fsdp')
- gate_up_grad: float32 [2, 6400, 2560], P(None, 'fsdp')
- down_proj_grad: float32 [6400, 2560], P('fsdp')
Inputs may be any that keep to these rules, and one draw needn't show every extreme that they name: `segment_ids`: segment numbers never fall along a sequence and each sequence holds the 4 documents 0 to 3, each of one token or more. Document 1 holds exactly 896 tokens and begins within the first 126 tokens; the others hold fewer than 128 tokens each.
All inputs are finite; a program needn't handle non-finite values.
Results may differ from a plain program's by a relative error of at most 0.023.
Values may be sent and summed in bfloat16 or wider, within the bound.
A program may use at most 768 MiB of HBM per device.

v0:
```python
import math

import jax
import jax.numpy as jnp
from jax import lax
from jax.sharding import PartitionSpec as P

D = 2560
H = 40
DN = 64
DR = 32
DV = 64
KR = 256


EPS = 1e-05
RESIDUAL_SCALE = 1.4 / math.sqrt(62.0)
NEGATIVE = -1e30
ROPE_BASE = 10000.0
HIGHEST = lax.Precision.HIGHEST


def normalize(values, gain):
    return values * lax.rsqrt(jnp.mean(values * values, axis=-1, keepdims=True) + EPS) * gain


def norm_back(values, gain, grad):
    primal, pullback = jax.vjp(normalize, values, gain)
    return pullback(grad)


def angles(positions, width):
    half = width // 2
    frequency = ROPE_BASE ** (-jnp.arange(half, dtype=jnp.float32) / half)
    theta = positions[:, None] * frequency[None, :]
    return (jnp.cos(theta), jnp.sin(theta))


def rotate(values, cosine, sine):
    half = values.shape[-1] // 2
    first = values[..., :half]
    second = values[..., half:]
    return jnp.concatenate(
        [first * cosine - second * sine, second * cosine + first * sine], axis=-1
    )


def unrotate(grad, cosine, sine):
    half = grad.shape[-1] // 2
    first = grad[..., :half]
    second = grad[..., half:]
    return jnp.concatenate(
        [first * cosine + second * sine, second * cosine - first * sine], axis=-1
    )


def swiglu_back(pre, grad_hidden):
    gate = pre[0]
    upper = pre[1]
    sigma = jax.nn.sigmoid(gate)
    return jnp.stack(
        [grad_hidden * upper * sigma * (1.0 + gate * (1.0 - sigma)), grad_hidden * gate * sigma],
        axis=0,
    )


def body(
    layer_input,
    segment_ids,
    attn_gain,
    query_down,
    query_gain,
    query_up,
    latent_down,
    latent_gain,
    latent_up,
    attn_output,
    ffn_gain,
    gate_up,
    down_proj,
    cotangent,
):
    f32 = jnp.float32
    bf16 = jnp.bfloat16
    span = layer_input.shape[1]
    seq_len = segment_ids.shape[1]
    offset = lax.axis_index(("ctx", "fsdp")) * span
    seg_all = segment_ids[0]
    seg_own = lax.dynamic_slice_in_dim(seg_all, offset, span, 0)
    index_own = offset + jnp.arange(span, dtype=jnp.int32)
    doc_start = jnp.sum((seg_all[None, :] < seg_own[:, None]).astype(jnp.int32), axis=1)
    cosine, sine = angles((index_own - doc_start).astype(f32), DR)
    inputs = layer_input[0].astype(f32)
    grad_out = cotangent[0].astype(f32)
    g_attn, w_qdown, g_query, w_qup, w_ldown, g_latent, w_lup, w_out, g_ffn = (
        lax.all_gather(attn_gain, "fsdp", axis=0, tiled=True),
        lax.all_gather(query_down, "fsdp", axis=0, tiled=True),
        lax.all_gather(query_gain, "fsdp", axis=0, tiled=True),
        lax.all_gather(query_up, "fsdp", axis=0, tiled=True),
        lax.all_gather(latent_down, "fsdp", axis=0, tiled=True),
        lax.all_gather(latent_gain, "fsdp", axis=0, tiled=True),
        lax.all_gather(latent_up, "fsdp", axis=0, tiled=True),
        lax.all_gather(attn_output, "fsdp", axis=0, tiled=True),
        lax.all_gather(ffn_gain, "fsdp", axis=0, tiled=True),
    )
    g_attn = g_attn.astype(f32)
    g_query = g_query.astype(f32)
    g_latent = g_latent.astype(f32)
    g_ffn = g_ffn.astype(f32)
    normed_in = normalize(inputs, g_attn).astype(bf16)
    query_latent = jnp.dot(normed_in, w_qdown, preferred_element_type=f32)
    query_normed = normalize(query_latent, g_query).astype(bf16)
    query_raw = jnp.dot(query_normed, w_qup, preferred_element_type=f32).reshape(span, H, DN + DR)
    queries = jnp.concatenate(
        [query_raw[..., :DN], rotate(query_raw[..., DN:], cosine[:, None, :], sine[:, None, :])],
        axis=-1,
    ).astype(bf16)
    latent_raw = jnp.dot(normed_in, w_ldown, preferred_element_type=f32)
    latent = normalize(latent_raw[:, :KR], g_latent).astype(bf16)
    key_rope = rotate(latent_raw[:, KR:], cosine, sine).astype(bf16)
    key_value = jnp.dot(latent, w_lup, preferred_element_type=f32).astype(bf16)
    key_value_all, key_rope_all = (
        lax.all_gather(key_value, ("ctx", "fsdp"), axis=0, tiled=True),
        lax.all_gather(key_rope, ("ctx", "fsdp"), axis=0, tiled=True),
    )
    key_value_all = key_value_all.reshape(seq_len, H, DN + DV)
    mask = (seg_own[:, None] == seg_all[None, :]) & (
        jnp.arange(seq_len, dtype=jnp.int32)[None, :] <= index_own[:, None]
    )
    scale = (DN + DR) ** (-0.5)
    group = 8

    def group_scores(first):
        query_part = queries[:, first : first + group]
        raw = jnp.einsum(
            "tgd,lgd->gtl",
            query_part[..., :DN],
            key_value_all[:, first : first + group, :DN],
            preferred_element_type=f32,
        )
        raw = raw + jnp.einsum(
            "tgd,ld->gtl", query_part[..., DN:], key_rope_all, preferred_element_type=f32
        )
        return jnp.where(mask[None], raw * scale, NEGATIVE)

    attended = []
    log_totals = []
    for head_block in range(H // group):
        first = head_block * group
        scores = group_scores(first)
        peak = jnp.max(scores, axis=-1, keepdims=True)
        weights = jnp.exp(scores - peak)
        denominator = jnp.sum(weights, axis=-1, keepdims=True)
        probs_low = (weights / denominator).astype(bf16)
        log_totals.append(peak + jnp.log(denominator))
        attended.append(
            jnp.einsum(
                "gtl,lgd->tgd",
                probs_low,
                key_value_all[:, first : first + group, DN:],
                preferred_element_type=f32,
            )
        )
    attn_out = jnp.concatenate(attended, axis=1).reshape(span, H * DV).astype(bf16)
    resid = inputs + RESIDUAL_SCALE * jnp.dot(attn_out, w_out, preferred_element_type=f32)
    ffn_in = normalize(resid, g_ffn).astype(bf16)
    grad_ffn = (RESIDUAL_SCALE * grad_out).astype(bf16)
    gate_and_up = jnp.einsum(
        "td,kfd->ktf",
        ffn_in,
        lax.all_gather(gate_up, "fsdp", axis=1, tiled=True),
        preferred_element_type=f32,
    )
    hidden = (jax.nn.silu(gate_and_up[0]) * gate_and_up[1]).astype(bf16)
    ffn_branch = jnp.dot(
        hidden, lax.all_gather(down_proj, "fsdp", axis=0, tiled=True), preferred_element_type=f32
    )
    grad_hidden = jnp.einsum(
        "td,fd->tf",
        grad_ffn,
        lax.all_gather(down_proj, "fsdp", axis=0, tiled=True),
        preferred_element_type=f32,
    )
    grad_gate_up = swiglu_back(gate_and_up, grad_hidden).astype(bf16)
    grad_ffn_in = jnp.einsum(
        "ktf,kfd->td",
        grad_gate_up,
        lax.all_gather(gate_up, "fsdp", axis=1, tiled=True),
        preferred_element_type=f32,
    )
    right_sides = jnp.stack([ffn_in, ffn_in, grad_ffn], axis=0)
    rows_own = gate_up.shape[1]
    left_sides = jnp.concatenate([grad_gate_up, hidden[None]], axis=0)
    terms = jnp.einsum("ktf,ktd->fkd", left_sides, right_sides, preferred_element_type=f32)
    combined = lax.psum_scatter(
        terms.reshape(rows_own * lax.axis_size("fsdp"), 3 * D).astype(jnp.bfloat16),
        "fsdp",
        scatter_dimension=0,
        tiled=True,
    ).astype(jnp.float32)
    gate_up_part = jnp.transpose(combined[:, : 2 * D].reshape(rows_own, 2, D), (1, 0, 2))
    down_part = combined[:, 2 * D :]
    output = resid + RESIDUAL_SCALE * ffn_branch
    grad_resid_add, ffn_gain_full = norm_back(resid, g_ffn, grad_ffn_in)
    grad_resid = grad_out + grad_resid_add
    grad_branch = (RESIDUAL_SCALE * grad_resid).astype(bf16)
    out_full = jnp.einsum("te,td->ed", attn_out, grad_branch, preferred_element_type=f32)
    grad_attn = (
        jnp.einsum("td,ed->te", grad_branch, w_out, preferred_element_type=f32)
        .astype(bf16)
        .reshape(span, H, DV)
    )
    grad_query_parts = []
    grad_key_parts = []
    grad_key_rope = jnp.zeros((seq_len, DR), f32)
    for head_block in range(H // group):
        first = head_block * group
        scores = group_scores(first)
        probs = jnp.exp(scores - log_totals[head_block])
        probs_low = probs.astype(bf16)
        query_part = queries[:, first : first + group]
        key_part = key_value_all[:, first : first + group, :DN]
        value_part = key_value_all[:, first : first + group, DN:]
        grad_part = grad_attn[:, first : first + group]
        grad_probs = jnp.einsum("tgd,lgd->gtl", grad_part, value_part, preferred_element_type=f32)
        delta = jnp.sum(probs * grad_probs, axis=-1, keepdims=True)
        grad_scores = (probs * (grad_probs - delta)).astype(bf16)
        grad_query_parts.append(
            jnp.concatenate(
                [
                    jnp.einsum("gtl,lgd->tgd", grad_scores, key_part, preferred_element_type=f32),
                    jnp.einsum(
                        "gtl,ld->tgd", grad_scores, key_rope_all, preferred_element_type=f32
                    ),
                ],
                axis=-1,
            )
            * scale
        )
        grad_key_parts.append(
            jnp.concatenate(
                [
                    jnp.einsum(
                        "gtl,tgd->lgd",
                        grad_scores,
                        query_part[..., :DN],
                        preferred_element_type=f32,
                    )
                    * scale,
                    jnp.einsum("gtl,tgd->lgd", probs_low, grad_part, preferred_element_type=f32),
                ],
                axis=-1,
            )
        )
        grad_key_rope = (
            grad_key_rope
            + jnp.einsum(
                "gtl,tgd->ld", grad_scores, query_part[..., DN:], preferred_element_type=f32
            )
            * scale
        )
    grad_queries = jnp.concatenate(grad_query_parts, axis=1)
    grad_key_value_all = jnp.concatenate(grad_key_parts, axis=1).reshape(seq_len, H * (DN + DV))
    lup_wide = w_lup.astype(f32)
    own_kv_grad, own_rope_grad = (
        lax.psum_scatter(
            grad_key_value_all.astype(jnp.bfloat16),
            ("ctx", "fsdp"),
            scatter_dimension=0,
            tiled=True,
        ).astype(jnp.float32),
        lax.psum_scatter(
            grad_key_rope.astype(jnp.bfloat16), ("ctx", "fsdp"), scatter_dimension=0, tiled=True
        ).astype(jnp.float32),
    )
    latent_up_full = jnp.dot(latent.astype(f32).T, own_kv_grad, precision=HIGHEST)
    grad_latent = jnp.dot(own_kv_grad, lup_wide.T, precision=HIGHEST)
    grad_latent_pre, latent_gain_full = norm_back(latent_raw[:, :KR], g_latent, grad_latent)
    grad_latent_raw = jnp.concatenate(
        [grad_latent_pre, unrotate(own_rope_grad, cosine, sine)], axis=-1
    ).astype(bf16)
    grad_query_raw = jnp.concatenate(
        [
            grad_queries[..., :DN],
            unrotate(grad_queries[..., DN:], cosine[:, None, :], sine[:, None, :]),
        ],
        axis=-1,
    )
    grad_query_raw = grad_query_raw.reshape(span, H * (DN + DR)).astype(bf16)
    query_up_full = jnp.einsum(
        "tq,tc->qc", query_normed, grad_query_raw, preferred_element_type=f32
    )
    grad_query_normed = jnp.einsum("tc,qc->tq", grad_query_raw, w_qup, preferred_element_type=f32)
    grad_query_pre, query_gain_full = norm_back(query_latent, g_query, grad_query_normed)
    grad_query_latent = grad_query_pre.astype(bf16)
    query_down_full = jnp.einsum(
        "td,tq->dq", normed_in, grad_query_latent, preferred_element_type=f32
    )
    latent_down_full = jnp.einsum(
        "td,tc->dc", normed_in, grad_latent_raw, preferred_element_type=f32
    )
    grad_normed_in = jnp.einsum("tq,dq->td", grad_query_latent, w_qdown, preferred_element_type=f32)
    grad_normed_in = grad_normed_in + jnp.einsum(
        "tc,dc->td", grad_latent_raw, w_ldown, preferred_element_type=f32
    )
    grad_input_add, attn_gain_full = norm_back(inputs, g_attn, grad_normed_in)
    input_grad = grad_resid + grad_input_add
    shards = (
        lax.psum_scatter(
            attn_gain_full.astype(jnp.bfloat16), "fsdp", scatter_dimension=0, tiled=True
        ).astype(jnp.float32),
        lax.psum_scatter(
            query_down_full.astype(jnp.bfloat16), "fsdp", scatter_dimension=0, tiled=True
        ).astype(jnp.float32),
        lax.psum_scatter(
            query_gain_full.astype(jnp.bfloat16), "fsdp", scatter_dimension=0, tiled=True
        ).astype(jnp.float32),
        lax.psum_scatter(
            query_up_full.astype(jnp.bfloat16), "fsdp", scatter_dimension=0, tiled=True
        ).astype(jnp.float32),
        lax.psum_scatter(
            latent_down_full.astype(jnp.bfloat16), "fsdp", scatter_dimension=0, tiled=True
        ).astype(jnp.float32),
        lax.psum_scatter(
            latent_gain_full.astype(jnp.bfloat16), "fsdp", scatter_dimension=0, tiled=True
        ).astype(jnp.float32),
        lax.psum_scatter(
            latent_up_full.astype(jnp.bfloat16), "fsdp", scatter_dimension=0, tiled=True
        ).astype(jnp.float32),
        lax.psum_scatter(
            out_full.astype(jnp.bfloat16), "fsdp", scatter_dimension=0, tiled=True
        ).astype(jnp.float32),
        lax.psum_scatter(
            ffn_gain_full.astype(jnp.bfloat16), "fsdp", scatter_dimension=0, tiled=True
        ).astype(jnp.float32),
    )
    totals = (
        lax.psum(shards[0].astype(jnp.bfloat16), ("dp", "ctx")).astype(jnp.float32),
        lax.psum(shards[1].astype(jnp.bfloat16), ("dp", "ctx")).astype(jnp.float32),
        lax.psum(shards[2].astype(jnp.bfloat16), ("dp", "ctx")).astype(jnp.float32),
        lax.psum(shards[3].astype(jnp.bfloat16), ("dp", "ctx")).astype(jnp.float32),
        lax.psum(shards[4].astype(jnp.bfloat16), ("dp", "ctx")).astype(jnp.float32),
        lax.psum(shards[5].astype(jnp.bfloat16), ("dp", "ctx")).astype(jnp.float32),
        lax.psum(shards[6].astype(jnp.bfloat16), ("dp", "ctx")).astype(jnp.float32),
        lax.psum(shards[7].astype(jnp.bfloat16), ("dp", "ctx")).astype(jnp.float32),
        lax.psum(shards[8].astype(jnp.bfloat16), ("dp", "ctx")).astype(jnp.float32),
        lax.psum(gate_up_part.astype(jnp.bfloat16), ("dp", "ctx")).astype(jnp.float32),
        lax.psum(down_part.astype(jnp.bfloat16), ("dp", "ctx")).astype(jnp.float32),
    )
    return (
        output.astype(bf16)[None],
        input_grad[None],
        totals[0],
        totals[1],
        totals[2],
        totals[3],
        totals[4],
        totals[5],
        totals[6],
        totals[7],
        totals[8],
        totals[9],
        totals[10],
    )


def solution(mesh):
    in_specs = (
        P("dp", ("ctx", "fsdp"), None),
        P("dp", None),
        P("fsdp"),
        P("fsdp", None),
        P("fsdp"),
        P("fsdp", None),
        P("fsdp", None),
        P("fsdp"),
        P("fsdp", None),
        P("fsdp", None),
        P("fsdp"),
        P(None, "fsdp", None),
        P("fsdp", None),
        P("dp", ("ctx", "fsdp"), None),
    )
    out_specs = (
        P("dp", ("ctx", "fsdp"), None),
        P("dp", ("ctx", "fsdp"), None),
        P("fsdp"),
        P("fsdp", None),
        P("fsdp"),
        P("fsdp", None),
        P("fsdp", None),
        P("fsdp"),
        P("fsdp", None),
        P("fsdp", None),
        P("fsdp"),
        P(None, "fsdp", None),
        P("fsdp", None),
    )
    return jax.shard_map(body, mesh=mesh, in_specs=in_specs, out_specs=out_specs, check_vma=False)
```

profile of v0, /device:TPU:0, one launch (start us, length us, event | category | flops | bytes accessed | tf_op | source)
XLA Modules:
  0.0 4089.9 jit_solution(8659486529819077662)
XLA Ops:
  10.1 6.1 all-gather
  18.7 8.0 all-reduce.10
  27.0 4.6 all-gather.11.cloned.1.call-done
  33.7 25.1 all-gather.13.cloned.1.call-done
  58.8 3.4 convolution_convert_fusion.4
  64.4 5.2 all-gather.1
  70.5 9.1 all_gather.49
  79.5 14.1 all-gather.17.cloned.1.call-done
  93.6 2.9 multiply_reduce_fusion.10
  96.6 42.6 %all-gather.19.cloned.1.call-done = bf16[768,3840]{1,0:T(8,128)(2,1)} async-done(((bf16[192,3840]{1,0:T(8,128)(2,1)}), bf16[768,3840]{1,0:T(8,128)(2,1)}) %all-gather.19.cloned.1.call-update) | async-done | bytes 5898256 | tf_op jit(solution)/shard_map/all_gather | solution.py:99
  139.2 5.2 fusion.244
  144.7 60.1 %all-gather.15.cloned.1.call-done = bf16[1024,5120]{1,0:T(8,128)(2,1)} async-done(((bf16[128,5120]{1,0:T(8,128)(2,1)}), bf16[1024,5120]{1,0:T(8,128)(2,1)}) %all-gather.15.cloned.1.call-update) | async-done | bytes 10485776 | tf_op jit(solution)/shard_map/all_gather | solution.py:123
  204.8 14.9 copy.113
  224.3 3.3 copy-done.10
  246.0 45.3 %all-gather.21.cloned.1.call-done = bf16[2560,2560]{1,0:T(8,128)(2,1)} async-done(((bf16[640,2560]{1,0:T(8,128)(2,1)}), bf16[2560,2560]{1,0:T(8,128)(2,1)}) %all-gather.21.cloned.1.call-update) | async-done | bytes 13107216 | tf_op jit(solution)/shard_map/all_gather | solution.py:103
  291.3 6.8 multiply_reduce_fusion.7
  298.2 378.5 %all-gather.23.cloned.1.call-done = bf16[2,6400,2560]{2,1,0:T(8,128)(2,1)} async-done(((bf16[2,1600,2560]{2,1,0:T(8,128)(2,1)}), bf16[2,6400,2560]{2,1,0:T(8,128)(2,1)}) %all-gather.23.cloned.1.call-update) | async-done | bytes 65536016 | tf_op jit(solution)/shard_map/all_gather | solution.py:171
  676.7 38.3 convolution_bitcast_fusion
  715.0 160.4 %all-gather.25.cloned.1.call-done = bf16[6400,2560]{1,0:T(8,128)(2,1)} async-done(((bf16[1600,2560]{1,0:T(8,128)(2,1)}), bf16[6400,2560]{1,0:T(8,128)(2,1)}) %all-gather.25.cloned.1.call-update) | async-done | bytes 32768016 | tf_op jit(solution)/shard_map/all_gather | solution.py:176
  875.5 18.5 fusion.70
  894.0 26.4 multiply_reduce_fusion.5
  924.1 9.0 convolution_convert_fusion.7
  933.5 4.3 multiply_reduce_fusion.4
  941.1 3.4 fusion.90
  944.5 4.7 multiply_reduce_fusion.3
  951.7 4.6 multiply_reduce_fusion.2
  958.9 3.3 multiply_reduce_fusion.1
  964.8 2.9 multiply_reduce_fusion
  969.6 3.2 multiply_convert_fusion.3
  974.9 3.1 multiply_convert_fusion.2
  987.2 3.0 maximum_dynamic-update-slice_fusion.4
  996.4 13.9 copy.107
  1012.3 3.8 multiply_convert_fusion.5
  1016.2 4.7 reduce-scatter.24.cloned.1.call-done
  1021.9 84.3 %reduce-scatter.22.cloned.1.call-done = bf16[128,5120]{1,0:T(8,128)(2,1)} async-done(((bf16[1024,5120]{1,0:T(8,128)(2,1)}), bf16[128,5120]{1,0:T(8,128)(2,1)}) %reduce-scatter.22.cloned.1.call-update) | async-done | bytes 1310736
  1106.2 3.5 multiply_reduce_fusion.11
  1111.7 3.8 copy.111
  1115.5 39.4 convolution_convert_fusion
  1154.9 111.8 %copy.97 = bf16[6400,7680]{1,0:T(8,128)(2,1)} copy(bf16[6400,7680]{0,1:T(8,128)(2,1)} %bitcast.59) | data formatting | bytes 196608000 | tf_op jit(solution)/shard_map/convert_element_type | solution.py:196
  1286.9 3.3 convolution_convert_fusion.5
  1290.3 4.4 convolution_convert_fusion.2
  1294.8 3.8 convolution_convert_fusion.3
  1298.7 6.8 convolution_convert_fusion.1
  1308.2 1558.6 %all-reduce.14.cloned.1.call-done = bf16[6400,7680]{1,0:T(8,128)(2,1)} async-done(((bf16[6400,7680]{1,0:T(8,128)(2,1)}), bf16[6400,7680]{1,0:T(8,128)(2,1)}) %all-reduce.14.cloned.1.call-update) | async-done | bytes 98304016
  2866.9 8.6 constant_dynamic-slice_fusion
  2875.4 6.8 copy.116
  2882.2 11.8 dynamic-slice.14
  2894.1 18.4 reduce-scatter.14.cloned.1.call-done
  2912.5 58.2 %reduce-scatter.16.cloned.1.call-done = bf16[192,3840]{1,0:T(8,128)(2,1)} async-done(((bf16[768,3840]{1,0:T(8,128)(2,1)}), bf16[192,3840]{1,0:T(8,128)(2,1)}) %reduce-scatter.16.cloned.1.call-update) | async-done | bytes 1474576 | tf_op jit(solution)/shard_map/reduce_scatter | solution.py:318
  2970.7 37.9 reduce-scatter.18.cloned.1.call-done
  3008.5 105.5 %reduce-scatter.20.cloned.1.call-done = bf16[640,2560]{1,0:T(8,128)(2,1)} async-done(((bf16[2560,2560]{1,0:T(8,128)(2,1)}), bf16[640,2560]{1,0:T(8,128)(2,1)}) %reduce-scatter.20.cloned.1.call-update) | async-done | bytes 3276816 | tf_op jit(solution)/shard_map/reduce_scatter | solution.py:330
  3116.0 4.5 fusion.260
  3120.6 19.4 fusion.23
  3140.1 3.6 fusion.111
  3143.7 11.2 all-reduce.9
  3155.2 23.3 all-reduce.7
  3180.7 2.8 fusion.115
  3183.5 866.1 %all-reduce.16.cloned.1.call-done = (bf16[640,768]{1,0:T(8,128)(2,1)}, bf16[192,3840]{1,0:T(8,128)(2,1)}, bf16[640,288]{0,1:T(8,128)(2,1)}, bf16[64,5120]{1,0:T(...) async-done(((bf16[640,768]{1,0:T(8,128)(2,1)}, bf16[192,3840]{1,0:T(8,128)(2,1)}, bf16[640,288]{0,1:T(8,128)(2,1)}, ...) | async-done | bytes 31334416 | tf_op jit(solution)/shard_map/psum | solution.py:339
  4049.6 2.8 convert_element_type.286
  4052.3 3.3 convert_element_type.290
  4056.6 3.0 convert_element_type.296
  4059.6 3.7 convert_element_type.298
  4063.2 11.5 convert_element_type.309
  4074.7 8.3 convert_element_type.310
  (341 shorter events, 97.2 us)
Async XLA Ops:
  7.2 9.1 copy-start.78
  7.2 11.0 copy-start.87
  7.2 11.3 copy-start.88
  7.2 19.5 copy-start.21
  7.2 24.4 all-gather.11.cloned.1.call-start
  8.0 50.8 %all-gather.13.cloned.1.call-start = ((), (), s32[]{:S(2)}) async-start(), calls=%async_computation.8 | async-start | bytes 3276800 | tf_op jit(solution)/shard_map/all_gather | solution.py:102
  8.7 84.9 %all-gather.17.cloned.1.call-start = ((), (), s32[]{:S(2)}) async-start(), calls=%async_computation.10 | async-start | bytes 4915200 | tf_op jit(solution)/shard_map/all_gather | solution.py:97
  9.4 129.8 %all-gather.19.cloned.1.call-start = ((), (), s32[]{:S(2)}) async-start(), calls=%async_computation.11 | async-start | bytes 7372800 | tf_op jit(solution)/shard_map/all_gather | solution.py:99
  10.0 194.8 %all-gather.15.cloned.1.call-start = ((), (), s32[]{:S(2)}) async-start(), calls=%async_computation.9 | async-start | bytes 11796480 | tf_op jit(solution)/shard_map/all_gather | solution.py:123
  16.3 77.3 %copy-start.48 = (f32[2560]{0:T(1024)}, f32[2560]{0:T(1024)S(1)}, u32[]{:S(2)}) copy-start(f32[2560]{0:T(1024)S(1)} %reshape.314) | copy-start | bytes 30724
  26.8 35.4 copy-start.59
  27.0 6.6 copy-start.85
  27.0 66.6 %copy-start.66 = (f32[128]{0:T(128)}, f32[128]{0:T(128)S(1)}, u32[]{:S(2)}) copy-start(f32[128]{0:T(128)S(1)} %fusion.227) | copy-start | bytes 1540
  33.6 36.6 copy-start.40
  33.6 29.1 copy-start.81
  33.7 29.1 copy-start.69
  62.2 229.1 %all-gather.21.cloned.1.call-start = ((), (), s32[]{:S(2)}) async-start(), calls=%async_computation.12 | async-start | bytes 16384000 | tf_op jit(solution)/shard_map/all_gather | solution.py:103
  62.8 613.9 %all-gather.23.cloned.1.call-start = ((), (), s32[]{:S(2)}) async-start(), calls=%async_computation.13 | async-start | bytes 81920000 | tf_op jit(solution)/shard_map/all_gather | solution.py:171
  63.6 6.1 copy-start.68
  63.6 811.9 %all-gather.25.cloned.1.call-start = ((), (), s32[]{:S(2)}) async-start(), calls=%async_computation.14 | async-start | bytes 40960000 | tf_op jit(solution)/shard_map/all_gather | solution.py:176
  64.3 956.5 %reduce-scatter.24.cloned.1.call-start = ((), (), s32[]{:S(2)}) async-start(), calls=%async_computation.20 | async-start | bytes 294912
  64.4 80.0 %copy-start.53 = (f32[768]{0:T(1024)}, f32[768]{0:T(1024)S(1)}, u32[]{:S(2)}) copy-start(f32[768]{0:T(1024)S(1)} %convert_element_type.249) | copy-start | bytes 9220
  70.3 74.3 %copy-start.55 = (f32[128,16]{0,1:T(8,128)}, f32[128,16]{0,1:T(8,128)S(1)}, u32[]{:S(2)}) copy-start(f32[128,16]{0,1:T(8,128)S(1)} %get-tuple-element.50) | copy-start | bytes 24580
  70.3 74.3 %copy-start.57 = (f32[128,16]{0,1:T(8,128)}, f32[128,16]{0,1:T(8,128)S(1)}, u32[]{:S(2)}) copy-start(f32[128,16]{0,1:T(8,128)S(1)} %get-tuple-element.51) | copy-start | bytes 24580
  79.5 158.1 %copy-start.28 = (bf16[1024,32]{0,1:T(8,128)(2,1)}, bf16[1024,32]{0,1:T(8,128)(2,1)S(1)}, u32[]{:S(2)}) copy-start(bf16[1024,32]{0,1:T(8,128)(2,1)S(1)} %all_gather.49) | copy-start | bytes 196612
  96.5 47.9 %copy-start.26 = (f32[128,768]{1,0:T(8,128)}, f32[128,768]{1,0:T(8,128)S(1)}, u32[]{:S(2)}) copy-start(f32[128,768]{1,0:T(8,128)S(1)} %get-tuple-element.55) | copy-start | bytes 1179652
  96.5 47.9 %copy-start.83 = (f32[128]{0:T(128)}, f32[128]{0:T(128)S(1)}, u32[]{:S(2)}) copy-start(f32[128]{0:T(128)S(1)} %get-tuple-element.54) | copy-start | bytes 1540
  96.6 47.9 %copy-start.71 = (f32[128]{0:T(128)}, f32[128]{0:T(128)S(1)}, u32[]{:S(2)}) copy-start(f32[128]{0:T(128)S(1)} %fusion.229) | copy-start | bytes 1540
  144.6 92.2 %copy-start.30 = (bf16[128,40,96]{0,2,1:T(8,128)(2,1)}, bf16[128,40,96]{0,2,1:T(8,128)(2,1)S(1)}, u32[]{:S(2)}) copy-start(bf16[128,40,96]{0,2,1:T(8,128)(2,1)S(1)} %convert.112) | copy-start | bytes 2949124
  223.2 17.1 copy-start.8
  229.6 11.9 copy-start.6
  232.6 9.9 copy-start.4
  235.7 8.0 copy-start.2
  246.0 52.1 %copy-start.32 = (bf16[128,40,64]{0,2,1:T(8,128)(2,1)}, bf16[128,40,64]{0,2,1:T(8,128)(2,1)S(1)}, u32[]{:S(2)}) copy-start(bf16[128,40,64]{0,2,1:T(8,128)(2,1)S(1)} %fusion.132) | copy-start | bytes 1966084
  298.1 622.3 %copy-start.24 = (f32[128,2560]{1,0:T(8,128)}, f32[128,2560]{1,0:T(8,128)S(1)}, u32[]{:S(2)}) copy-start(f32[128,2560]{1,0:T(8,128)S(1)} %get-tuple-element.67) | copy-start | bytes 3932164
  676.7 198.7 %copy-start.42 = (bf16[1,128,2560]{2,1,0:T(8,128)(2,1)S(1)}, bf16[1,128,2560]{2,1,0:T(8,128)(2,1)}, u32[]{:S(2)}) copy-start(bf16[1,128,2560]{2,1,0:T(8,128)(2,1)} %param.27) | copy-start | bytes 1966084
  940.6 8.6 copy-start.11
  987.1 119.1 %reduce-scatter.22.cloned.1.call-start = ((), (), s32[]{:S(2)}) async-start(), calls=%async_computation.19 | async-start | bytes 11796480
  1010.3 296.0 %reduce-scatter.26.cloned.1.call-start = ((), (), s32[]{:S(2)}) async-start(), calls=%async_computation.21 | async-start | bytes 2457600
  1012.3 9.4 copy-start.74
  1012.3 9.4 copy-start.76
  1012.3 93.9 %copy-start.41 = (f32[128,288]{0,1:T(8,128)S(1)}, f32[128,288]{0,1:T(8,128)}, u32[]{:S(2)}) copy-start(f32[128,288]{0,1:T(8,128)} %copy-done.40) | copy-start | bytes 442372
  1012.3 93.9 %copy-start.60 = (f32[256]{0:T(256)S(1)}, f32[256]{0:T(256)}, u32[]{:S(2)}) copy-start(f32[256]{0:T(256)} %copy-done.59) | copy-start | bytes 3076
  1012.3 93.9 %copy-start.70 = (f32[128]{0:T(128)S(1)}, f32[128]{0:T(128)}, u32[]{:S(2)}) copy-start(f32[128]{0:T(128)} %copy-done.69) | copy-start | bytes 1540
  1016.2 93.6 %copy-start.82 = (f32[128]{0:T(128)S(1)}, f32[128]{0:T(128)}, u32[]{:S(2)}) copy-start(f32[128]{0:T(128)} %copy-done.81) | copy-start | bytes 1540
  1016.2 93.7 %copy-start.49 = (f32[2560]{0:T(1024)S(1)}, f32[2560]{0:T(1024)}, u32[]{:S(2)}) copy-start(f32[2560]{0:T(1024)} %copy-done.48) | copy-start | bytes 30724
  1016.2 93.7 %copy-start.67 = (f32[128]{0:T(128)S(1)}, f32[128]{0:T(128)}, u32[]{:S(2)}) copy-start(f32[128]{0:T(128)} %copy-done.66) | copy-start | bytes 1540
  1021.8 89.8 %copy-start.61 = (bf16[128,16]{0,1:T(8,128)(2,1)}, bf16[128,16]{0,1:T(8,128)(2,1)S(1)}, u32[]{:S(2)}) copy-start(bf16[128,16]{0,1:T(8,128)(2,1)S(1)} %get-tuple-element.48) | copy-start | bytes 12292
  1021.9 89.8 %copy-start.63 = (bf16[128,16]{0,1:T(8,128)(2,1)}, bf16[128,16]{0,1:T(8,128)(2,1)S(1)}, u32[]{:S(2)}) copy-start(bf16[128,16]{0,1:T(8,128)(2,1)S(1)} %get-tuple-element.49) | copy-start | bytes 12292
  1115.4 1751.4 %all-reduce.14.cloned.1.call-start = ((), (), s32[]{:S(2)}) async-start(), calls=%async_computation.22 | async-start | bytes 196608000
  1266.7 1645.8 %reduce-scatter.14.cloned.1.call-start = ((), (), s32[]{:S(2)}) async-start(), calls=%async_computation.15 | async-start | bytes 4915200 | tf_op jit(solution)/shard_map/reduce_scatter | solution.py:312
  1290.2 1680.4 %reduce-scatter.16.cloned.1.call-start = ((), (), s32[]{:S(2)}) async-start(), calls=%async_computation.16 | async-start | bytes 7372800 | tf_op jit(solution)/shard_map/reduce_scatter | solution.py:318
  1294.7 1713.8 %reduce-scatter.18.cloned.1.call-start = ((), (), s32[]{:S(2)}) async-start(), calls=%async_computation.17 | async-start | bytes 3276800 | tf_op jit(solution)/shard_map/reduce_scatter | solution.py:327
  1298.6 1815.5 %reduce-scatter.20.cloned.1.call-start = ((), (), s32[]{:S(2)}) async-start(), calls=%async_computation.18 | async-start | bytes 16384000 | tf_op jit(solution)/shard_map/reduce_scatter | solution.py:330
  1305.5 2744.0 %all-reduce.16.cloned.1.call-start = ((), (), s32[]{:S(2)}) async-start(), calls=%async_computation.23 | async-start | bytes 62668800 | tf_op jit(solution)/shard_map/psum | solution.py:339
  3120.6 19.4 copy-start.51
  3120.6 19.4 copy-start.62
  3120.6 19.4 copy-start.64
  3140.1 40.7 copy-start.86
  4049.6 6.1 copy-start.52
  4049.6 10.0 copy-start.39
  4052.3 10.9 copy-start.25
  4059.6 15.2 slice-start.2
  4063.2 11.5 slice-start.3
  (46 other events, 133.9 us)
Sparse Core Ops, SparseCore 0:
  9.6 21.9 all-gather.10
  33.1 25.5 all-gather.12
  60.3 33.2 all-gather.16
  95.0 44.1 all-gather.18
  141.5 63.2 all-gather.14
  206.2 85.0 all-gather.20
  292.9 383.7 all-gather.22
  678.3 197.1 all-gather.24
  987.2 33.6 reduce-scatter.23
  1024.6 81.5 reduce-scatter.21
  1115.6 30.6 reduce-scatter.25
  1266.8 1599.9 all-reduce.13
  2869.6 42.8 reduce-scatter.13
  2914.9 55.7 reduce-scatter.15
  2973.8 34.6 reduce-scatter.17
  3011.6 102.4 reduce-scatter.19
  3120.9 928.6 all-reduce.15
where the time goes:
time: 4100 us; the launch traced here: 4090 us
  waiting for transfers between devices  3470 us (85%)
  matrix products  279 us (7%)
  local copies, waits for them, and re-layouts  187 us (5%)
  other arithmetic  71.4 us (2%)
  blocking collectives  62.8 us (2%)
    unnamed x21, waiting for transfers between devices  1650 us
    psum x1, waiting for transfers between devices, body(): lax.psum(shards[1].astype(jnp.bfloat16), ('dp', 'ctx')).astype(jnp.float32)  866 us
    all_gather x1, waiting for transfers between devices, body(): lax.all_gather(gate_up, 'fsdp', axis=1, tiled=True)  379 us
    all_gather x1, waiting for transfers between devices, body(): lax.all_gather(down_proj, 'fsdp', axis=0, tiled=True)  160 us
    convert_element_type x1, local copies, waits for them, and re-layouts, body(): terms.reshape(rows_own * lax.axis_size('fsdp'), 3 * D).astype(jnp.bfloat16)  112 us
    reduce_scatter x1, waiting for transfers between devices, body(): lax.psum_scatter(out_full.astype(jnp.bfloat16), 'fsdp', scatter_dimension...  106 us
  transfers between devices with their start and end apart: 17, of which 16 were waited for; matrix products, arithmetic and copies ran while one was open for 9% of the time, Pallas kernels for 0%

commit v1 on v0

v1 whole, which is shorter than its diff:
```python
import functools
import math

import jax
import jax.numpy as jnp
import numpy as np
from jax import lax
from jax.experimental import pallas as pl
from jax.experimental.pallas import tpu as pltpu
from jax.sharding import PartitionSpec as P

D = 2560
H = 40
DN = 64
DR = 32
DV = 64
QR = 768
KR = 256
LANES = 128
DOWN = QR + KR + DR
PACK = QR + KR + LANES
EXTRA = 32

EPS = 1e-05
RESIDUAL_SCALE = 1.4 / math.sqrt(62.0)
NEGATIVE = -1e30
ROPE_BASE = 10000.0
SCALE = (DN + DR) ** (-0.5)
f32 = jnp.float32
bf16 = jnp.bfloat16

NN = (((1,), (0,)), ((), ()))
NT = (((1,), (1,)), ((), ()))
TN = (((0,), (0,)), ((), ()))
MIB = 1024 * 1024


def dot(left, right, dims=NN):
    return lax.dot_general(left, right, dims, preferred_element_type=f32)


def normalize(values, gain):
    return values * lax.rsqrt(jnp.mean(values * values, axis=-1, keepdims=True) + EPS) * gain


def norm_back(values, gain, grad):
    primal, pullback = jax.vjp(normalize, values, gain)
    return pullback(grad)


def angles(positions):
    half = DR // 2
    frequency = ROPE_BASE ** (-jnp.arange(half, dtype=f32) / half)
    theta = positions[:, None] * frequency[None, :]
    return (jnp.cos(theta), jnp.sin(theta))


def rotate(values, cosine, sine):
    half = values.shape[-1] // 2
    first = values[..., :half]
    second = values[..., half:]
    return jnp.concatenate(
        [first * cosine - second * sine, second * cosine + first * sine], axis=-1
    )


def unrotate(grad, cosine, sine):
    return rotate(grad, cosine, -sine)


def swapped(values):
    lane = lax.broadcasted_iota(jnp.int32, values.shape, 1)
    up = pltpu.roll(values, LANES - DR // 2, 1)
    back = pltpu.roll(values, DR // 2, 1)
    return jnp.where(lane < DN + DR // 2, up, -back)


def allowed(seg_col, seg_row, first, rows, columns):
    query = first + lax.broadcasted_iota(jnp.int32, (rows, columns), 0)
    key = lax.broadcasted_iota(jnp.int32, (rows, columns), 1)
    return (seg_col[first : first + rows, :] == seg_row[:, :columns]) & (key <= query)


PLANE = ("ctx", "fsdp")
ALL = ("dp", "ctx", "fsdp")
MESH = pl.DeviceIdType.MESH


def seats():
    y = lax.axis_index("ctx")
    f = lax.axis_index("fsdp")
    core = lax.rem(f, 2)
    mate = {"fsdp": f + 1 - 2 * core}
    along_x = {"fsdp": lax.rem(f + 2, 4)}
    along_y = {"ctx": 1 - y}
    return y, f, core, mate, along_x, along_y


def greet(peers):
    barrier = pltpu.get_barrier_semaphore()
    for peer in peers:
        pl.semaphore_signal(barrier, inc=1, device_id=peer, device_id_type=MESH)
    pl.semaphore_wait(barrier, len(peers))


class Wires:
    def __init__(self, send, recv):
        self.send, self.recv, self.count = send, recv, 0

    def copy(self, src, dst, peer):
        at = self.count
        self.count += 1
        return pltpu.make_async_remote_copy(
            src_ref=src,
            dst_ref=dst,
            send_sem=self.send.at[at],
            recv_sem=self.recv.at[at],
            device_id=peer,
            device_id_type=MESH,
        )


class Spread:
    wires_needed = 9

    def __init__(self, wires, src, out, base, local):
        rows = src.shape[0]
        half = rows // 2
        y, f, core, mate, along_x, along_y = seats()
        x_f = lax.rem(f + 2, 4)
        me, x_seat, y_seat, far = y * 4 + f, y * 4 + x_f, (1 - y) * 4 + f, (1 - y) * 4 + x_f
        at = lambda seat, first, count: out.at[
            pl.ds(pl.multiple_of(base + seat * rows + first, 16), count)
        ]
        whole = lambda seat: at(seat, 0, rows)
        upper = lambda seat: at(seat, 0, half)
        lower = lambda seat: at(seat, half, half)
        self.keep = pltpu.make_async_copy(src, whole(me), local)
        self.mine = [wires.copy(src, whole(me), peer) for peer in (along_x, along_y, mate)]
        self.pass_y = wires.copy(upper(x_seat), upper(x_seat), along_y)
        self.pass_x = wires.copy(lower(y_seat), lower(y_seat), along_x)
        self.mate_x = wires.copy(whole(x_seat), whole(x_seat), mate)
        self.mate_y = wires.copy(whole(y_seat), whole(y_seat), mate)
        self.mate_u = wires.copy(upper(far), upper(far), mate)
        self.mate_l = wires.copy(lower(far), lower(far), mate)

    def start(self):
        for copy in self.mine:
            copy.start()
        self.keep.start()

    def relay(self):
        self.mine[0].wait_recv()
        self.pass_y.start()
        self.mate_x.start()
        self.mine[1].wait_recv()
        self.pass_x.start()
        self.mate_y.start()

    def finish(self):
        self.pass_y.wait_recv()
        self.mate_u.start()
        self.pass_x.wait_recv()
        self.mate_l.start()
        for copy in (self.mine[2], self.mate_x, self.mate_y, self.mate_u, self.mate_l):
            copy.wait_recv()
        rest = [self.pass_y, self.pass_x, self.mate_x, self.mate_y, self.mate_u, self.mate_l]
        for copy in self.mine + rest:
            copy.wait_send()
        self.keep.wait()


class Light:
    wires_needed = 6

    def __init__(self, wires, src, far_src, stage, out, base, local):
        rows = src.shape[0]
        y, f, core, mate, along_x, along_y = seats()
        x_f = lax.rem(f + 2, 4)
        me, x_seat, y_seat, far = y * 4 + f, y * 4 + x_f, (1 - y) * 4 + f, (1 - y) * 4 + x_f
        at = lambda seat: out.at[pl.ds(pl.multiple_of(base + seat * rows, 16), rows)]
        self.fetch = [
            pltpu.make_async_copy(src, stage.at[0], local.at[0]),
            pltpu.make_async_copy(far_src, stage.at[1], local.at[1]),
        ]
        self.keep = [
            pltpu.make_async_copy(stage.at[0], at(me), local.at[2]),
            pltpu.make_async_copy(stage.at[1], at(far), local.at[3]),
        ]
        self.mine = [wires.copy(stage.at[0], at(me), peer) for peer in (along_x, along_y, mate)]
        self.far = wires.copy(stage.at[1], at(far), mate)
        self.mate_x = wires.copy(at(x_seat), at(x_seat), mate)
        self.mate_y = wires.copy(at(y_seat), at(y_seat), mate)

    def load(self):
        for copy in self.fetch:
            copy.start()

    def start(self):
        for copy in self.fetch:
            copy.wait()
        for copy in self.mine + [self.far] + self.keep:
            copy.start()

    def relay(self):
        self.mine[0].wait_recv()
        self.mate_x.start()
        self.mine[1].wait_recv()
        self.mate_y.start()

    def finish(self):
        for copy in (self.mine[2], self.far, self.mate_x, self.mate_y):
            copy.wait_recv()
        for copy in self.mine + [self.far, self.mate_x, self.mate_y]:
            copy.wait_send()
        for copy in self.keep:
            copy.wait()


def turn_z(step):
    return lax.rem(lax.axis_index("dp") + step, lax.axis_size("dp"))


def attend_kernel(
    block, units, lat, wq, wl, cos, sin, seg_col, seg_row, *rest
):
    sources, rest = rest[:units], rest[units:]
    (q_out, k_out, kv_out, o_out, lse_out), rest = rest[:5], rest[5:]
    length = lat.shape[0]
    if units:
        out, local, send, recv = rest
        unit = Spread(Wires(send, recv), sources[0], out, 0, local.at[0])

        @pl.when(pl.program_id(0) == 0)
        def _():
            seat = seats()
            greet(seat[3:])
            unit.start()

        @pl.when(pl.program_id(0) == 3)
        def _():
            unit.relay()

    lane = lax.broadcasted_iota(jnp.int32, (length, LANES), 1)
    query = dot(lat[:, :QR], wq[...])
    query = (query * cos[...] - swapped(query) * sin[...]).astype(bf16)
    both = dot(lat[:, QR : QR + KR], wl[...]).astype(bf16)
    key = jnp.where(lane < DN, both, lat[:, QR + KR :])
    q_out[...] = query
    k_out[...] = key
    kv_out[...] = both
    for first in range(0, length, block):
        last = first + block
        scores = dot(query[first:last], key[:last], NT) * SCALE
        scores = jnp.where(allowed(seg_col, seg_row, first, block, last), scores, NEGATIVE)
        peak = jnp.max(scores, axis=-1, keepdims=True)
        weights = jnp.exp(scores - peak)
        total = jnp.sum(weights, axis=-1, keepdims=True)
        probs = (weights * (1.0 / total)).astype(bf16)
        o_out[first:last, :] = dot(probs, both[:last]).astype(bf16)
        lse_out[0, first:last, :] = peak + jnp.log(total)
    if units:

        @pl.when(pl.program_id(0) == pl.num_programs(0) - 1)
        def _():
            unit.finish()


def attend(lat, wq, wl, cos, sin, seg_col, seg_row, cot=None, tokens=0, name_id=0):
    length = lat.shape[0]
    heads = wq.shape[1] // LANES
    whole = lambda shape: pl.BlockSpec(shape, lambda h: (0,) * len(shape))
    mine = lambda rows: pl.BlockSpec((rows, LANES), lambda h: (0, h))
    anywhere = [pl.BlockSpec(memory_space=pl.ANY)]
    wide = jax.ShapeDtypeStruct((length, heads * LANES), bf16)
    units = 0 if cot is None else 1
    wires = Spread.wires_needed
    params = dict(collective_id=name_id, has_side_effects=True) if units else {}
    return pl.pallas_call(
        functools.partial(attend_kernel, min(256, length), units),
        grid=(heads,),
        in_specs=[
            whole((length, PACK)),
            mine(QR),
            mine(KR),
            whole((length, LANES)),
            whole((length, LANES)),
            whole((length, 1)),
            whole((1, length)),
        ]
        + [whole((length // 8, D))] * units,
        out_specs=[mine(length)] * 4
        + [pl.BlockSpec((1, length, 1), lambda h: (h, 0, 0))]
        + anywhere * units,
        out_shape=[wide] * 4
        + [jax.ShapeDtypeStruct((heads, length, 1), f32)]
        + [jax.ShapeDtypeStruct((tokens, D), bf16)] * units,
        scratch_shapes=[
            pltpu.SemaphoreType.DMA((1,)),
            pltpu.SemaphoreType.DMA((wires,)),
            pltpu.SemaphoreType.DMA((wires,)),
        ]
        if units
        else [],
        compiler_params=pltpu.CompilerParams(vmem_limit_bytes=56 * MIB, **params),
        cost_estimate=pl.CostEstimate(
            flops=heads * length * (length * 4 * LANES + 2 * LANES * (QR + KR)),
            bytes_accessed=heads * length * LANES * 16,
            transcendentals=heads * length * length,
        ),
    )(lat, wq, wl, cos, sin, seg_col, seg_row, *([cot] if units else []))


def attend_back_kernel(
    block, units, gb, wo, q, k, kv, o, lse, cos, sin, seg_col, seg_row, *rest
):
    sources, rest = rest[: 5 * units], rest[5 * units :]
    (gq_out, gkv_out, rope_out, wo_out), rest = rest[:4], rest[4:]
    length = gb.shape[0]
    if units:
        x_z, cot_z, cot_far, _, _ = sources
        x_all, cot_all, dk, dv, stage, local, send, recv = rest
        wires = Wires(send, recv)
        z = turn_z(1)
        fetch = pltpu.make_async_copy(x_z.at[z], stage.at[2], local.at[5])
        first_unit = Spread(wires, stage.at[2], x_all, length, local.at[4])
        second_unit = Light(
            wires, cot_z.at[z], cot_far.at[z], stage, cot_all, length, local
        )

        @pl.when(pl.program_id(0) == 0)
        def _():
            fetch.start()
            second_unit.load()
            seat = seats()
            greet(seat[3:])
            fetch.wait()
            first_unit.start()
            second_unit.start()

        @pl.when(pl.program_id(0) == 3)
        def _():
            first_unit.relay()
            second_unit.relay()

    else:
        dk, dv = rest
    wo_out[...] = dot(o[...], gb[...], TN)[LANES - DV :].astype(bf16)
    lane = lax.broadcasted_iota(jnp.int32, (length, LANES), 1)
    grad = dot(gb[...], wo[...], NT).astype(bf16)
    dk[...] = jnp.zeros_like(dk)
    dv[...] = jnp.zeros_like(dv)
    for first in range(0, length, block):
        last = first + block
        scores = dot(q[first:last, :], k[:last, :], NT) * SCALE
        probs = jnp.exp(scores - lse[0, first:last, :])
        probs = jnp.where(allowed(seg_col, seg_row, first, block, last), probs, 0.0)
        grad_probs = dot(grad[first:last], kv[:last, :], NT)
        delta = jnp.sum(probs * grad_probs, axis=-1, keepdims=True)
        grad_scores = (probs * (grad_probs - delta)).astype(bf16)
        gq = dot(grad_scores, k[:last, :]) * SCALE
        gq = gq * cos[first:last, :] + swapped(gq) * sin[first:last, :]
        gq_out[first:last, :] = gq.astype(bf16)
        dk[:last, :] += dot(grad_scores, q[first:last, :], TN) * SCALE
        dv[:last, :] += dot(probs.astype(bf16), grad[first:last], TN)
    gkv_out[...] = jnp.where(lane < DN, dk[...], dv[...]).astype(bf16)

    @pl.when(pl.program_id(0) == 0)
    def _():
        rope_out[...] = dk[...]

    @pl.when(pl.program_id(0) > 0)
    def _():
        rope_out[...] += dk[...]

    if units:

        @pl.when(pl.program_id(0) == pl.num_programs(0) - 1)
        def _():
            first_unit.finish()
            second_unit.finish()


def attend_back(gb, wo, q, k, kv, o, lse, cos, sin, seg_col, seg_row, bulk=(), tokens=0, name_id=0):
    units = 1 if bulk else 0
    wires = Spread.wires_needed + Light.wires_needed
    anywhere = [pl.BlockSpec(memory_space=pl.ANY)]
    params = dict(collective_id=name_id, has_side_effects=True) if units else {}
    length = gb.shape[0]
    heads = q.shape[1] // LANES
    whole = lambda shape: pl.BlockSpec(shape, lambda h: (0,) * len(shape))
    mine = pl.BlockSpec((length, LANES), lambda h: (0, h))
    wide = jax.ShapeDtypeStruct((length, heads * LANES), bf16)
    return pl.pallas_call(
        functools.partial(attend_back_kernel, min(256, length), units),
        grid=(heads,),
        in_specs=[
            whole((length, D)),
            pl.BlockSpec((LANES, D), lambda h: (h, 0)),
            mine,
            mine,
            mine,
            mine,
            pl.BlockSpec((1, length, 1), lambda h: (h, 0, 0)),
            whole((length, LANES)),
            whole((length, LANES)),
            whole((length, 1)),
            whole((1, length)),
        ]
        + anywhere * (5 * units),
        out_specs=[
            mine,
            mine,
            whole((length, LANES)),
            pl.BlockSpec((DV, D), lambda h: (h, 0)),
        ]
        + anywhere * (2 * units),
        input_output_aliases={14: 4, 15: 5} if units else {},
        out_shape=[
            wide,
            wide,
            jax.ShapeDtypeStruct((length, LANES), f32),
            jax.ShapeDtypeStruct((heads * DV, D), bf16),
        ]
        + [jax.ShapeDtypeStruct((tokens, D), bf16)] * (2 * units),
        scratch_shapes=[pltpu.VMEM((length, LANES), f32), pltpu.VMEM((length, LANES), f32)]
        + [
            pltpu.VMEM((3, length // 8, D), bf16),
            pltpu.SemaphoreType.DMA((6,)),
            pltpu.SemaphoreType.DMA((wires,)),
            pltpu.SemaphoreType.DMA((wires,)),
        ]
        * units,
        compiler_params=pltpu.CompilerParams(vmem_limit_bytes=56 * MIB, **params),
        cost_estimate=pl.CostEstimate(
            flops=heads * length * (length * 10 * LANES + 4 * LANES * D),
            bytes_accessed=heads * length * LANES * 16 + length * D * 2,
            transcendentals=heads * length * length,
        ),
    )(gb, wo, q, k, kv, o, lse, cos, sin, seg_col, seg_row, *bulk)


def hidden_block(x, cot, w_gu, w_down, h_out, g_out, parts):
    units = w_down.shape[0]
    step = units // parts
    for part in range(parts):
        rows = slice(part * step, (part + 1) * step)
        gate = dot(w_gu[0, rows, :], x, NT)
        upper = dot(w_gu[1, rows, :], x, NT)
        grad = dot(w_down[rows, :], cot, NT) * RESIDUAL_SCALE
        sigma = jax.nn.sigmoid(gate)
        silu = gate * sigma
        h_out[rows, :] = (silu * upper).astype(bf16)
        g_out[0, rows, :] = (grad * upper * sigma * (1.0 + gate * (1.0 - sigma))).astype(bf16)
        g_out[1, rows, :] = (grad * silu).astype(bf16)


def ffn_own_kernel(place, x, cot, w_gu, w_down, h_out, g_out, y_out, gx_out):
    hidden_block(x[...], cot[...], w_gu, w_down, h_out, g_out, 2)
    y_out[...] = dot(h_out[...], w_down[...], TN).astype(bf16)
    gx_out[...] = (dot(g_out[0], w_gu[0], TN) + dot(g_out[1], w_gu[1], TN)).astype(bf16)


def ffn_rest_kernel(place, x, cot, w_gu, w_down, h_in, g_in, h_out, g_out):
    hidden_block(x[...], cot[...], w_gu, w_down, h_out, g_out, 2)


def ffn_shapes(units, tokens):
    return [
        jax.ShapeDtypeStruct((units, tokens), bf16),
        jax.ShapeDtypeStruct((2, units, tokens), bf16),
    ]


def ffn_own(place, x, cot_all, w_gu, w_down):
    units = w_down.shape[0]
    tokens = cot_all.shape[0]
    block = min(256, x.shape[0])
    steps = x.shape[0] // block
    kept = pl.Buffered(1)
    return pl.pallas_call(
        ffn_own_kernel,
        grid_spec=pltpu.PrefetchScalarGridSpec(
            num_scalar_prefetch=1,
            grid=(steps,),
            in_specs=[
                pl.BlockSpec((block, D), lambda i, p: (i, 0)),
                pl.BlockSpec((block, D), lambda i, p: (p[0] * steps + i, 0)),
                pl.BlockSpec((2, units, D), lambda i, p: (0, 0, 0), pipeline_mode=kept),
                pl.BlockSpec((units, D), lambda i, p: (0, 0), pipeline_mode=kept),
            ],
            out_specs=[
                pl.BlockSpec((units, block), lambda i, p: (0, p[0] * steps + i)),
                pl.BlockSpec((2, units, block), lambda i, p: (0, 0, p[0] * steps + i)),
                pl.BlockSpec((block, D), lambda i, p: (i, 0)),
                pl.BlockSpec((block, D), lambda i, p: (i, 0)),
            ],
        ),
        out_shape=ffn_shapes(units, tokens) + [jax.ShapeDtypeStruct((x.shape[0], D), bf16)] * 2,
        compiler_params=pltpu.CompilerParams(vmem_limit_bytes=60 * MIB),
        cost_estimate=pl.CostEstimate(
            flops=12 * x.shape[0] * units * D, bytes_accessed=6 * units * D, transcendentals=0
        ),
    )(place, x, cot_all, w_gu, w_down)


def ffn_rest(place, x_all, cot_all, w_gu, w_down, h_all, g_all, own):
    units = w_down.shape[0]
    tokens = x_all.shape[0]
    block = min(256, own)
    steps = own // block
    blocks = tokens // block
    kept = pl.Buffered(1)
    at = lambda i, p: lax.rem((p[0] + 1) * steps + i, blocks)
    return pl.pallas_call(
        ffn_rest_kernel,
        grid_spec=pltpu.PrefetchScalarGridSpec(
            num_scalar_prefetch=1,
            grid=(blocks - steps,),
            in_specs=[
                pl.BlockSpec((block, D), lambda i, p: (at(i, p), 0)),
                pl.BlockSpec((block, D), lambda i, p: (at(i, p), 0)),
                pl.BlockSpec((2, units, D), lambda i, p: (0, 0, 0), pipeline_mode=kept),
                pl.BlockSpec((units, D), lambda i, p: (0, 0), pipeline_mode=kept),
                pl.BlockSpec(memory_space=pl.ANY),
                pl.BlockSpec(memory_space=pl.ANY),
            ],
            out_specs=[
                pl.BlockSpec((units, block), lambda i, p: (0, at(i, p))),
                pl.BlockSpec((2, units, block), lambda i, p: (0, 0, at(i, p))),
            ],
        ),
        out_shape=ffn_shapes(units, tokens),
        input_output_aliases={5: 0, 6: 1},
        compiler_params=pltpu.CompilerParams(vmem_limit_bytes=60 * MIB),
        cost_estimate=pl.CostEstimate(
            flops=6 * (tokens - own) * units * D,
            bytes_accessed=6 * units * D + 10 * tokens * D,
            transcendentals=0,
        ),
    )(place, x_all, cot_all, w_gu, w_down, h_all, g_all)


def remote_call(kernel, name_id, out_shape, scratch, wires, operands):
    return pl.pallas_call(
        kernel,
        out_shape=out_shape,
        in_specs=[pl.BlockSpec(memory_space=pltpu.VMEM)] * len(operands),
        out_specs=jax.tree.map(lambda _: pl.BlockSpec(memory_space=pltpu.VMEM), out_shape),
        scratch_shapes=scratch
        + [pltpu.SemaphoreType.DMA((wires,)), pltpu.SemaphoreType.DMA((wires,))],
        compiler_params=pltpu.CompilerParams(
            collective_id=name_id, has_side_effects=True, vmem_limit_bytes=56 * MIB
        ),
    )(*operands)


def gather_plane_steps(wires, x, out):
    rows = x.shape[0]
    half = rows // 2
    y, f, core, mate, along_x, along_y = seats()
    me = y * 4 + f
    x_seat = y * 4 + lax.rem(f + 2, 4)
    y_seat = (1 - y) * 4 + f
    far = (1 - y) * 4 + lax.rem(f + 2, 4)
    whole = lambda seat: out.at[pl.ds(seat * rows, rows)]
    upper = lambda seat: out.at[pl.ds(seat * rows, half)]
    lower = lambda seat: out.at[pl.ds(seat * rows + half, half)]
    mine_x = wires.copy(x, whole(me), along_x)
    mine_y = wires.copy(x, whole(me), along_y)
    mine_m = wires.copy(x, whole(me), mate)
    mine_x.start()
    mine_y.start()
    mine_m.start()
    out[pl.ds(me * rows, rows), :] = x[...]
    pass_y = wires.copy(upper(x_seat), upper(x_seat), along_y)
    pass_x = wires.copy(lower(y_seat), lower(y_seat), along_x)
    mate_x = wires.copy(whole(x_seat), whole(x_seat), mate)
    mate_y = wires.copy(whole(y_seat), whole(y_seat), mate)
    mate_u = wires.copy(upper(far), upper(far), mate)
    mate_l = wires.copy(lower(far), lower(far), mate)
    mine_x.wait_recv()
    pass_y.start()
    mate_x.start()
    mine_y.wait_recv()
    pass_x.start()
    mate_y.start()
    pass_y.wait_recv()
    mate_u.start()
    pass_x.wait_recv()
    mate_l.start()
    for copy in (mine_m, mate_x, mate_y, mate_u, mate_l):
        copy.wait_recv()
    for copy in (mine_x, mine_y, mine_m, pass_y, pass_x, mate_x, mate_y, mate_u, mate_l):
        copy.wait_send()


def plane_gather_kernel(x, out, send, recv):
    y, f, core, mate, along_x, along_y = seats()
    greet([mate, along_x, along_y])
    gather_plane_steps(Wires(send, recv), x, out)


def plane_gather(x, name_id):
    shape = jax.ShapeDtypeStruct((8 * x.shape[0], x.shape[1]), x.dtype)
    return remote_call(plane_gather_kernel, name_id, shape, [], 9, (x,))


def scatter_plane_steps(wires, part, out, own, from_mate, from_x, from_y, last, relay, fill=None):
    rows = out.shape[0]
    half = rows // 2
    y, f, core, mate, along_x, along_y = seats()
    x_f = lax.rem(f + 2, 4)
    turn = 1 - 2 * core
    seat = [(1 - y) * 4 + x_f, y * 4 + x_f, (1 - y) * 4 + f, y * 4 + f]
    upper, lower = slice(0, half), slice(half, rows)
    to_mate = [
        wires.copy(part.at[pl.ds((s + turn) * rows, rows)], from_mate.at[i], mate)
        for i, s in enumerate(seat)
    ]
    for copy in to_mate:
        copy.start()
    far_x = wires.copy(own.at[0, upper], from_x.at[0], along_x)
    far_y = wires.copy(own.at[0, lower], from_y.at[0], along_y)
    near_x = wires.copy(own.at[1, upper], from_x.at[1], along_x)
    near_y = wires.copy(own.at[2, lower], from_y.at[1], along_y)
    relay_y = wires.copy(relay.at[0], last.at[0], along_y)
    relay_x = wires.copy(relay.at[1], last.at[1], along_x)
    starts = ([far_x, far_y], [near_x], [near_y], [])
    for i in range(4):
        to_mate[i].wait_recv()
        own[i] = part[pl.ds(seat[i] * rows, rows), :] + from_mate[i]
        for copy in starts[i]:
            copy.start()
    if fill is not None:
        fill()
    far_x.wait_recv()
    relay[0] = own[2, upper] + from_x[0]
    relay_y.start()
    far_y.wait_recv()
    relay[1] = own[1, lower] + from_y[0]
    relay_x.start()
    near_x.wait_recv()
    near_y.wait_recv()
    relay_y.wait_recv()
    relay_x.wait_recv()
    add = lambda a, b, c: (a.astype(f32) + b.astype(f32) + c.astype(f32)).astype(out.dtype)
    out[upper, :] = add(own[3, upper], from_x[1], last[0])
    out[lower, :] = add(own[3, lower], from_y[1], last[1])
    for copy in to_mate + [far_x, far_y, near_x, near_y, relay_y, relay_x]:
        copy.wait_send()


def plane_scatter_kernel(part, out, own, from_mate, from_x, from_y, last, relay, send, recv):
    greet(seats()[3:])
    wires = Wires(send, recv)
    scatter_plane_steps(wires, part, out, own, from_mate, from_x, from_y, last, relay)


def plane_scatter(part, name_id):
    rows, width = part.shape[0] // 8, part.shape[1]
    shape = jax.ShapeDtypeStruct((rows, width), part.dtype)
    buffer = lambda count, depth: pltpu.VMEM((count, depth, width), part.dtype)
    scratch = [buffer(4, rows), buffer(4, rows)] + [buffer(2, rows // 2)] * 4
    return remote_call(plane_scatter_kernel, name_id, shape, scratch, 10, (part,))


def take_columns(weight, first, width):
    begin = min(first // LANES * LANES, weight.shape[1] - 2 * LANES)
    window = weight[:, begin : begin + 2 * LANES].astype(f32)
    shift = (2 * LANES - (first - begin)) % (2 * LANES)
    window = (pltpu.roll(window, shift, 1) if shift else window)[:, :LANES]
    lane = lax.broadcasted_iota(jnp.int32, window.shape, 1)
    return jnp.where(lane < width, window, 0.0).astype(bf16)


def front_kernel(
    pieces,
    heads,
    x,
    qd,
    ld,
    gain_a,
    gain_f,
    gain_q,
    gain_l,
    qup,
    lup,
    seg_col,
    seg_row,
    freq,
    lat,
    wq,
    wl,
    w_in,
    raw_out,
    n_out,
    gains_out,
    cos_out,
    sin_out,
    w,
    gains,
    gains_all,
    qpack,
    own,
    send,
    recv,
):
    rows = w.shape[0]
    half = rows // 2
    piece = half // pieces
    span = x.shape[0]
    length = cos_out.shape[0]
    y, f, core, mate, along_x, along_y = seats()
    x_f = lax.rem(f + 2, 4)
    m_f = f + 1 - 2 * core
    c_f = 3 - f
    cross = {"fsdp": c_f}
    wires = Wires(send, recv)

    w[:, :QR] = qd[...]
    w[:, QR:] = jnp.zeros((rows, PACK - QR), bf16)
    w[:, QR:DOWN] = ld[...]
    gains[...] = jnp.zeros_like(gains)
    gains[0:1, : gain_a.shape[1]] = gain_a[...].astype(f32)
    gains[1:2, : gain_f.shape[1]] = gain_f[...].astype(f32)
    gains[2:3, : gain_q.shape[1]] = gain_q[...].astype(f32)
    gains[3:4, : gain_l.shape[1]] = gain_l[...].astype(f32)
    greet([mate, along_x, along_y, cross])

    gains_x = wires.copy(gains, gains_all.at[f], along_x)
    gains_m = wires.copy(gains, gains_all.at[f], mate)
    gains_r = wires.copy(gains_all.at[x_f], gains_all.at[x_f], mate)
    spot = lambda owner, side, i: pl.ds(owner * rows + side * half + i * piece, piece)
    across = [
        wires.copy(w.at[pl.ds(y * half + i * piece, piece)], w_in.at[spot(f, y, i)], along_x)
        for i in range(pieces)
    ]
    mine = wires.copy(w, w_in.at[pl.ds(f * rows, rows)], mate)
    same = lambda side, peer: [
        wires.copy(w_in.at[spot(x_f, side, i)], w_in.at[spot(x_f, side, i)], peer)
        for i in range(pieces)
    ]
    trade = same(y, along_y)
    to_mate = same(y, mate)
    rest = same(1 - y, mate)
    gains_x.start()
    gains_m.start()
    for copy in across:
        copy.start()
    mine.start()
    gains_all[f] = gains[...]
    w_in[pl.ds(f * rows, rows), :] = w[...]

    q_rows, l_rows = qup.shape[0], lup.shape[0]
    for seat in range(4):
        for head in range(heads):
            first = lambda ctx: ((seat * 2 + ctx) * heads + head) * (DN + DR)
            column = jnp.where(
                y == 0,
                take_columns(qup, first(0), DN + DR).astype(f32),
                take_columns(qup, first(1), DN + DR).astype(f32),
            )
            qpack[seat, :, head * LANES : (head + 1) * LANES] = column.astype(bf16)
    width = heads * LANES
    kv_part = lambda seat: lup.at[:, pl.ds(pl.multiple_of((seat * 2 + y) * width, LANES), width)]
    q_spot = wq.at[pl.ds(f * q_rows, q_rows)]
    l_spot = wl.at[pl.ds(f * l_rows, l_rows)]
    swaps = []
    for seat, peer in ((x_f, along_x), (c_f, cross), (m_f, mate)):
        swaps.append(wires.copy(qpack.at[seat], q_spot, peer))
        swaps.append(wires.copy(kv_part(seat), l_spot, peer))
    for copy in swaps:
        copy.start()
    wq[pl.ds(f * q_rows, q_rows), :] = qpack[f]
    wl[pl.ds(f * l_rows, l_rows), :] = lup[
        :, pl.ds(pl.multiple_of((f * 2 + y) * width, LANES), width)
    ]

    index = lax.broadcasted_iota(jnp.int32, (length, 1), 0).astype(f32)
    seg = seg_col[...]
    doc_start = jnp.zeros((length, 1), f32)
    for number in range(1, 4):
        start = jnp.sum((seg_row[...] < number).astype(f32), axis=1, keepdims=True)
        doc_start = jnp.where(seg == number, start, doc_start)
    theta = (index - doc_start) * freq[...]
    lane = lax.broadcasted_iota(jnp.int32, (length, LANES), 1)
    turned = (lane >= DN) & (lane < DN + DR)
    cos_out[...] = jnp.where(turned, jnp.cos(theta), jnp.where(lane < DN, 1.0, 0.0))
    sin_out[...] = jnp.where(turned, jnp.sin(theta), 0.0)

    gains_x.wait_recv()
    gains_r.start()
    gains_m.wait_recv()
    gains_r.wait_recv()
    shard = gain_a.shape[1]
    full = [gains_all[i] for i in range(4)]
    g_attn = jnp.concatenate([full[i][0:1, :shard] for i in range(4)], axis=1)
    g_ffn = jnp.concatenate([full[i][1:2, :shard] for i in range(4)], axis=1)
    placed = [full[0]]
    for i in range(1, 4):
        placed.append(pltpu.roll(full[i], i * gain_q.shape[1], 1))
    g_query = sum(p[2:3] for p in placed)
    placed = [full[0]]
    for i in range(1, 4):
        placed.append(pltpu.roll(full[i], i * gain_l.shape[1], 1))
    g_latent = sum(p[3:4] for p in placed)[:, :KR]
    gains_out[...] = jnp.zeros_like(gains_out)
    gains_out[0:1, :] = g_attn
    gains_out[1:2, :] = g_ffn
    gains_out[2:3, :QR] = g_query
    gains_out[3:4, :KR] = g_latent

    inputs = x[...].astype(f32)
    n_out[...] = normalize(inputs, g_attn).astype(bf16)

    def term(owner):
        left = n_out[:, pl.ds(pl.multiple_of(owner * rows, LANES), rows)]
        return dot(left, w_in[pl.ds(owner * rows, rows), :])

    raw_out[...] = term(f)
    for i in range(pieces):
        across[i].wait_recv()
        trade[i].start()
        to_mate[i].start()
    mine.wait_recv()
    raw_out[...] += term(m_f)
    for i in range(pieces):
        trade[i].wait_recv()
        rest[i].start()
    raw_out[...] += term(x_f)
    for copy in to_mate + rest:
        copy.wait_recv()
    raw_out[...] += term(c_f)

    me = y * 4 + f
    cos = cos_out[pl.ds(me * span, span), :]
    sin = sin_out[pl.ds(me * span, span), :]
    own[:, :QR] = normalize(raw_out[:, :QR], g_query).astype(bf16)
    own[:, QR : QR + KR] = normalize(raw_out[:, QR : QR + KR], g_latent).astype(bf16)
    rope = pltpu.roll(raw_out[:, QR + KR :], DN, 1)
    own[:, QR + KR :] = (rope * cos - swapped(rope) * sin).astype(bf16)
    gather_plane_steps(wires, own, lat)

    for copy in swaps:
        copy.wait_recv()
    for copy in [gains_x, gains_m, gains_r, mine] + across + trade + to_mate + rest + swaps:
        copy.wait_send()


def front(x, qd, ld, gains, qup, lup, seg_col, seg_row, heads, name_id):
    freq = ROPE_BASE ** (-np.arange(DR // 2, dtype=np.float32) / (DR // 2))
    freq = np.concatenate([np.zeros(DN), freq, freq, np.zeros(LANES - DN - DR)])
    freq = jnp.asarray(freq[None], f32)
    span, length = x.shape[0], seg_col.shape[0]
    rows, width = qd.shape[0], heads * LANES
    shape = jax.ShapeDtypeStruct
    shapes = (
        shape((length, PACK), bf16),
        shape((QR, width), bf16),
        shape((KR, width), bf16),
        shape((4 * rows, PACK), bf16),
        shape((span, PACK), f32),
        shape((span, D), bf16),
        shape((8, D), f32),
        shape((length, LANES), f32),
        shape((length, LANES), f32),
    )
    pieces = 4
    scratch = [
        pltpu.VMEM((rows, PACK), bf16),
        pltpu.VMEM((8, QR), f32),
        pltpu.VMEM((4, 8, QR), f32),
        pltpu.VMEM((4, qup.shape[0], width), bf16),
        pltpu.VMEM((span, PACK), bf16),
    ]
    operands = (x, qd, ld) + tuple(g[None] for g in gains) + (qup, lup, seg_col, seg_row, freq)
    return remote_call(
        functools.partial(front_kernel, pieces, heads),
        name_id,
        shapes,
        scratch,
        4 + 4 * pieces + 6 + 9,
        operands,
    )


def ffn_group_kernel(
    columns,
    x,
    cot_all,
    w_gu,
    w_down,
    h_out,
    g_out,
    gx_out,
    y_keep,
    y_send,
    x_all,
    wg,
    wd,
    xs,
    cs,
    hv,
    gv,
    ht,
    gt,
    gx_part,
    y_part,
    g_mate,
    y_mate,
    sent,
    from_x,
    local,
    send,
    recv,
):
    units = wd.shape[0]
    span = x.shape[0]
    block = 2 * span
    width = D // columns
    y, f, core, mate, along_x, along_y = seats()
    group = y * 4 * span
    chip = lax.div(f, 2)
    load_gu = pltpu.make_async_copy(w_gu, wg, local.at[0])
    load_down = pltpu.make_async_copy(w_down, wd, local.at[1])
    load_gu.start()
    load_down.start()
    load_cot = []
    for at, which in enumerate((chip, 1 - chip)):
        where = pl.ds(pl.multiple_of(group + which * block, LANES), block)
        load_cot.append(pltpu.make_async_copy(cot_all.at[where], cs.at[at], local.at[6 + at]))
        load_cot[at].start()
    greet([mate, along_x, along_y])
    wires = Wires(send, recv)
    x_f = lax.rem(f + 2, 4)
    me, y_seat, far = y * 4 + f, (1 - y) * 4 + f, (1 - y) * 4 + x_f
    half = span // 2
    place = lambda seat, first, rows: x_all.at[
        pl.ds(pl.multiple_of(seat * span + first, 16), rows)
    ]
    mine = pl.ds(core * span, span)
    other = pl.ds((1 - core) * span, span)
    x_x = wires.copy(x, xs.at[1, mine], along_x)
    x_m = wires.copy(x, xs.at[0, mine], mate)
    x_x.start()
    x_m.start()
    xs[0, mine] = x[...]
    x_r = wires.copy(xs.at[1, mine], xs.at[1, mine], mate)
    x_y = wires.copy(x, place(me, 0, span), along_y)
    x_y.start()
    pass_y = wires.copy(
        xs.at[1, pl.ds(core * span, half)], place(y * 4 + x_f, 0, half), along_y
    )
    pass_x = wires.copy(place(y_seat, half, half), place(y_seat, half, half), along_x)
    mate_y = wires.copy(place(y_seat, 0, span), place(y_seat, 0, span), mate)
    mate_u = wires.copy(place(far, 0, half), place(far, 0, half), mate)
    mate_l = wires.copy(place(far, half, half), place(far, half, half), mate)
    keep_x = [
        pltpu.make_async_copy(
            xs.at[at], place(y * 4 + which * 2, 0, block), local.at[8 + at]
        )
        for at, which in enumerate((chip, 1 - chip))
    ]
    y_m = [wires.copy(y_part.at[i, other], y_mate.at[i], mate) for i in range(2)]
    cols = [slice(i * width, (i + 1) * width) for i in range(columns)]
    to_mate = lambda at: [
        wires.copy(gx_part.at[at, other, c], g_mate.at[at, :, c], mate) for c in cols
    ]
    g_near, g_far = to_mate(0), to_mate(1)
    g_x = [wires.copy(sent.at[:, c], from_x.at[:, c], along_x) for c in cols]

    cut = units // 2 // LANES * LANES

    def hidden(at):
        tokens = slice(at * block, (at + 1) * block)
        for rows in (slice(0, cut), slice(cut, units)):
            gate = dot(wg[0, rows, :], xs[at], NT)
            upper = dot(wg[1, rows, :], xs[at], NT)
            grad = dot(wd[rows, :], cs[at], NT) * RESIDUAL_SCALE
            sigma = jax.nn.sigmoid(gate)
            silu = gate * sigma
            value = silu * upper
            hv[at, rows, :] = value.astype(bf16)
            ht[tokens, rows] = value.T.astype(bf16)
            value = grad * upper * sigma * (1.0 + gate * (1.0 - sigma))
            gv[at, 0, rows, :] = value.astype(bf16)
            gt[0, tokens, rows] = value.T.astype(bf16)
            value = grad * silu
            gv[at, 1, rows, :] = value.astype(bf16)
            gt[1, tokens, rows] = value.T.astype(bf16)
        which = chip if at == 0 else 1 - chip
        where = pl.ds(pl.multiple_of(group + which * block, LANES), block)
        out_h = pltpu.make_async_copy(hv.at[at], h_out.at[:, where], local.at[2 + 2 * at])
        out_g = pltpu.make_async_copy(gv.at[at], g_out.at[:, :, where], local.at[3 + 2 * at])
        out_h.start()
        out_g.start()
        return [out_h, out_g]

    load_gu.wait()
    load_down.wait()
    x_m.wait_recv()
    for copy in load_cot:
        copy.wait()
    stores = hidden(0)
    x_x.wait_recv()
    x_r.start()
    pass_y.start()
    x_y.wait_recv()
    pass_x.start()
    mate_y.start()
    x_r.wait_recv()
    for copy in keep_x:
        copy.start()
    stores += hidden(1) + keep_x

    def pass_on(i):
        g_far[i].wait_recv()
        sent[:, cols[i]] = gx_part[1, mine, cols[i]] + g_mate[1, :, cols[i]]
        g_x[i].start()

    for i, c in enumerate(cols):
        total = dot(gt[0], wg[0, :, c]) + dot(gt[1], wg[1, :, c])
        gx_part[:, :, c] = total.astype(bf16).reshape(2, block, width)
        g_far[i].start()
        g_near[i].start()
        if i > 0:
            pass_on(i - 1)
    pass_y.wait_recv()
    mate_u.start()
    pass_x.wait_recv()
    mate_l.start()
    for i, c in enumerate(cols):
        y_part[:, :, c] = dot(ht[...], wd[:, c]).astype(bf16).reshape(2, block, width)
        if i == 0:
            pass_on(columns - 1)
    for copy in y_m:
        copy.start()
    for i, c in enumerate(cols):
        g_near[i].wait_recv()
        g_x[i].wait_recv()
        keep = gx_part[0, mine, c].astype(f32) + g_mate[0, :, c].astype(f32)
        gx_out[:, c] = (keep + from_x[:, c].astype(f32)).astype(bf16)
    for copy in y_m:
        copy.wait_recv()
    y_keep[...] = y_part[0, mine] + y_mate[0]
    y_send[...] = y_part[1, mine] + y_mate[1]
    for copy in (mate_y, mate_u, mate_l):
        copy.wait_recv()
    plane = [x_y, pass_y, pass_x, mate_y, mate_u, mate_l]
    for copy in [x_x, x_m, x_r] + y_m + g_near + g_far + g_x + plane:
        copy.wait_send()
    for copy in stores:
        copy.wait()


def ffn_group(x, cot_all, w_gu, w_down, name_id):
    tokens = cot_all.shape[0]
    span = x.shape[0]
    units = w_down.shape[0]
    columns = 5
    wires = 11 + 3 * columns
    anywhere = pl.BlockSpec(memory_space=pl.ANY)
    vmem = pl.BlockSpec(memory_space=pltpu.VMEM)
    buffer = lambda *shape: pltpu.VMEM(shape, bf16)
    return pl.pallas_call(
        functools.partial(ffn_group_kernel, columns),
        out_shape=ffn_shapes(units, tokens)
        + [jax.ShapeDtypeStruct((span, D), bf16)] * 3
        + [jax.ShapeDtypeStruct((tokens, D), bf16)],
        in_specs=[vmem, anywhere, anywhere, anywhere],
        out_specs=[anywhere, anywhere, vmem, vmem, vmem, anywhere],
        scratch_shapes=[
            buffer(2, units, D),
            buffer(units, D),
            buffer(2, 2 * span, D),
            buffer(2, 2 * span, D),
            buffer(2, units, 2 * span),
            buffer(2, 2, units, 2 * span),
            buffer(4 * span, units),
            buffer(2, 4 * span, units),
            buffer(2, 2 * span, D),
            buffer(2, 2 * span, D),
            buffer(2, span, D),
            buffer(2, span, D),
            buffer(span, D),
            buffer(span, D),
            pltpu.SemaphoreType.DMA((10,)),
            pltpu.SemaphoreType.DMA((wires,)),
            pltpu.SemaphoreType.DMA((wires,)),
        ],
        compiler_params=pltpu.CompilerParams(
            collective_id=name_id, has_side_effects=True, vmem_limit_bytes=62 * MIB
        ),
        cost_estimate=pl.CostEstimate(
            flops=12 * 4 * span * units * D, bytes_accessed=6 * units * D, transcendentals=0
        ),
    )(x, cot_all, w_gu, w_down)


def ffn_others_kernel(
    span,
    x_z,
    cot_z,
    x_far,
    cot_far,
    x_in,
    cot_in,
    h_in,
    g_in,
    w_gu,
    w_down,
    x_all,
    cot_all,
    h_out,
    g_out,
    wg,
    wd,
    xb,
    cb,
    hb,
    gb,
    stage,
    loads,
    local,
    slots_in,
    slots_out,
    send,
    recv,
):
    length = 8 * span
    block = 2 * span
    y = lax.axis_index("ctx")
    load_gu = pltpu.make_async_copy(w_gu, wg, loads.at[0])
    load_down = pltpu.make_async_copy(w_down, wd, loads.at[1])
    load_gu.start()
    load_down.start()
    greet(seats()[3:])
    wires = Wires(send, recv)
    def unit(r, own, far, out, at):
        z = turn_z(r)
        return Light(
            wires, own.at[z], far.at[z], stage.at[at], out, r * length, local.at[at]
        )

    x_unit = {r: unit(r, x_z, x_far, x_all, r - 2) for r in (2, 3)}
    c_unit = {r: unit(r, cot_z, cot_far, cot_all, r) for r in (2, 3)}
    for one in (x_unit[2], c_unit[2], x_unit[3], c_unit[3]):
        one.load()
    x_unit[2].start()
    c_unit[2].start()

    def where(i):
        first = jnp.where(i < 2, (1 - y) * 4 * span + i * block, length + (i - 2) * block)
        return pl.ds(pl.multiple_of(first, LANES), block)

    def fetch(i):
        slot = lax.rem(i, 2)
        return [
            pltpu.make_async_copy(x_all.at[where(i)], xb.at[slot], slots_in.at[0, slot]),
            pltpu.make_async_copy(cot_all.at[where(i)], cb.at[slot], slots_in.at[1, slot]),
        ]

    def store(i):
        slot = lax.rem(i, 2)
        return [
            pltpu.make_async_copy(hb.at[slot], h_out.at[:, where(i)], slots_out.at[0, slot]),
            pltpu.make_async_copy(gb.at[slot], g_out.at[:, :, where(i)], slots_out.at[1, slot]),
        ]

    count = 14
    for copy in fetch(0):
        copy.start()
    load_gu.wait()
    load_down.wait()

    def step(i, carry):
        slot = lax.rem(i, 2)
        for copy in fetch(i):
            copy.wait()

        @pl.when(i >= 2)
        def _():
            for copy in store(i - 2):
                copy.wait()

        def between(number, *steps):
            @pl.when(i == number)
            def _():
                for one in steps:
                    one()

        between(3, x_unit[2].relay, c_unit[2].relay, x_unit[3].start)
        between(4, c_unit[3].start)
        between(5, x_unit[2].finish, c_unit[2].finish)
        between(8, x_unit[3].relay, c_unit[3].relay)
        between(9, x_unit[3].finish, c_unit[3].finish)

        @pl.when(i + 1 < count)
        def _():
            for copy in fetch(i + 1):
                copy.start()

        hidden_block(xb[slot], cb[slot], wg, wd, hb.at[slot], gb.at[slot], 2)
        for copy in store(i):
            copy.start()
        return carry

    lax.fori_loop(0, count, step, 0)
    for i in (count - 2, count - 1):
        for copy in store(i):
            copy.wait()


def ffn_others(x_z, cot_z, x_far, cot_far, x_all, cot_all, h_all, g_all, w_gu, w_down, name_id):
    units = w_down.shape[0]
    tokens = x_all.shape[0]
    span = x_z.shape[1]
    block = 2 * span
    wires = 4 * Light.wires_needed
    anywhere = pl.BlockSpec(memory_space=pl.ANY)
    buffer = lambda *shape: pltpu.VMEM(shape, bf16)
    return pl.pallas_call(
        functools.partial(ffn_others_kernel, span),
        out_shape=[jax.ShapeDtypeStruct((tokens, D), bf16)] * 2 + ffn_shapes(units, tokens),
        in_specs=[anywhere] * 10,
        out_specs=[anywhere] * 4,
        input_output_aliases={4: 0, 5: 1, 6: 2, 7: 3},
        scratch_shapes=[
            buffer(2, units, D),
            buffer(units, D),
            buffer(2, block, D),
            buffer(2, block, D),
            buffer(2, units, block),
            buffer(2, 2, units, block),
            buffer(4, 2, span, D),
            pltpu.SemaphoreType.DMA((2,)),
            pltpu.SemaphoreType.DMA((4, 4)),
            pltpu.SemaphoreType.DMA((2, 2)),
            pltpu.SemaphoreType.DMA((2, 2)),
            pltpu.SemaphoreType.DMA((wires,)),
            pltpu.SemaphoreType.DMA((wires,)),
        ],
        compiler_params=pltpu.CompilerParams(
            collective_id=name_id, has_side_effects=True, vmem_limit_bytes=60 * MIB
        ),
        cost_estimate=pl.CostEstimate(
            flops=6 * (tokens - 4 * span) * units * D,
            bytes_accessed=6 * units * D + 10 * tokens * D,
            transcendentals=0,
        ),
    )(x_z, cot_z, x_far, cot_far, x_all, cot_all, h_all, g_all, w_gu, w_down)


def norm_back_rows(values, gain, grad):
    inverse = lax.rsqrt(jnp.mean(values * values, axis=-1, keepdims=True) + EPS)
    unit = values * inverse
    scaled = gain * grad
    return (scaled - unit * jnp.mean(unit * scaled, axis=-1, keepdims=True)) * inverse


def finish_kernel(
    gq,
    gkv,
    rope,
    lat,
    wq,
    wl,
    w_in,
    raw,
    n,
    x,
    grad_resid,
    gains,
    cos_all,
    sin_all,
    ffn_gain,
    part,
    input_grad,
    lat_part,
    lat_sum,
    own,
    from_mate,
    from_x,
    from_y,
    last,
    relay,
    n_all,
    ups,
    raw_own,
    raw_all,
    down,
    traded,
    send,
    recv,
):
    span = x.shape[0]
    length = gq.shape[0]
    width = gq.shape[1]
    rows = w_in.shape[0] // 4
    q_rows, l_rows = QR // 4, KR // 4
    y, f, core, mate, along_x, along_y = seats()
    x_f, m_f, c_f = lax.rem(f + 2, 4), f + 1 - 2 * core, 3 - f
    cross = {"fsdp": c_f}
    others = ((x_f, along_x), (c_f, cross), (m_f, mate))
    greet([mate, along_x, along_y, cross])
    wires = Wires(send, recv)
    columns = lambda seat: pl.ds(pl.multiple_of(seat * rows, LANES), rows)
    mine = pl.ds(f * span, span)
    n_sends = [wires.copy(n.at[:, columns(seat)], n_all.at[mine], peer) for seat, peer in others]
    for copy in n_sends:
        copy.start()
    n_all[mine, :] = n[:, columns(f)]

    each = span + EXTRA
    for first in range(0, length, 512):
        some = slice(first, first + 512)
        q_part = dot(gq[some, :], wq[...], NT).astype(bf16)
        l_part = dot(gkv[some, :], wl[...], NT).astype(bf16)
        r_part = rope[some, :].astype(bf16)
        for at in range(0, 512, span):
            here = (first + at) // span * each
            lat_part[here : here + span, :QR] = q_part[at : at + span]
            lat_part[here : here + span, QR : QR + KR] = l_part[at : at + span]
            lat_part[here : here + span, QR + KR :] = r_part[at : at + span]
    for seat in range(8):
        here = seat * each + span
        piece = ffn_gain[:, seat % 4 * rows : (seat % 4 + 1) * rows]
        lat_part[here : here + EXTRA, :] = jnp.zeros((EXTRA, PACK), bf16)
        lat_part[here : here + EXTRA, :rows] = jnp.broadcast_to(piece, (EXTRA, rows)).astype(bf16)

    swap_rows = q_rows + l_rows
    swaps = [
        wires.copy(ups.at[seat], part.at[pl.ds(f * swap_rows, swap_rows)], peer)
        for seat, peer in others
    ]

    def column_gradients():
        q_grad = dot(lat[:, :QR], gq[...], TN).astype(bf16)
        l_grad = dot(lat[:, QR : QR + KR], gkv[...], TN).astype(bf16)
        for seat in range(4):
            ups[seat, :q_rows] = q_grad[seat * q_rows : (seat + 1) * q_rows]
            ups[seat, q_rows:] = l_grad[seat * l_rows : (seat + 1) * l_rows]
        part[pl.ds(f * swap_rows, swap_rows), :] = ups[f]

    scatter_plane_steps(
        wires, lat_part, lat_sum, own, from_mate, from_x, from_y, last, relay, column_gradients
    )

    me = pl.ds((y * 4 + f) * span, span)
    grad = lat_sum[:span, :].astype(f32)
    raw_own[:, :QR] = norm_back_rows(raw[:, :QR], gains[2:3, :QR], grad[:, :QR]).astype(bf16)
    raw_own[:, QR : QR + KR] = norm_back_rows(
        raw[:, QR : QR + KR], gains[3:4, :KR], grad[:, QR : QR + KR]
    ).astype(bf16)
    turned = grad[:, QR + KR :]
    lane = lax.broadcasted_iota(jnp.int32, turned.shape, 1)
    turned = turned * cos_all[me, :] + swapped(turned) * sin_all[me, :]
    turned = jnp.where((lane >= DN) & (lane < DN + DR), turned, 0.0)
    raw_own[:, QR + KR :] = pltpu.roll(turned, LANES - DN, 1).astype(bf16)
    raw_x = wires.copy(raw_own, raw_all.at[mine], along_x)
    raw_m = wires.copy(raw_own, raw_all.at[mine], mate)
    theirs = raw_all.at[pl.ds(x_f * span, span)]
    raw_r = wires.copy(theirs, theirs, mate)
    raw_x.start()
    raw_m.start()
    for copy in swaps:
        copy.start()
    raw_all[mine, :] = raw_own[...]
    for copy in n_sends:
        copy.wait_recv()
    raw_x.wait_recv()
    raw_r.start()
    raw_m.wait_recv()
    raw_r.wait_recv()

    down[...] = dot(n_all[...], raw_all[...], TN).astype(bf16)
    half = rows // 2
    trade = wires.copy(down.at[pl.ds((1 - y) * half, half)], traded, along_y)
    trade.start()
    inputs = x[...].astype(f32)
    grad_in = dot(raw_own[...], w_in[...], NT)
    input_grad[...] = grad_resid[...] + norm_back_rows(inputs, gains[0:1, :], grad_in)
    first = 4 * swap_rows
    last_rows = part.shape[0] - first - 2 * half
    part[first + 2 * half :, :] = jnp.zeros((last_rows, width), bf16)
    part[first + 2 * half :, :rows] = lat_sum[span : span + last_rows, :rows]
    trade.wait_recv()
    kept = down[pl.ds(y * half, half), :] + traded[...]
    part[first : first + half, :] = kept[:, :width]
    part[first + half : first + 2 * half, :] = jnp.zeros((half, width), bf16)
    part[first + half : first + 2 * half, : PACK - width] = kept[:, width:]
    for copy in swaps:
        copy.wait_recv()
    for copy in n_sends + swaps + [raw_x, raw_m, raw_r, trade]:
        copy.wait_send()


def finish(operands, name_id):
    gq, x, w_in = operands[0], operands[9], operands[6]
    span, width, rows = x.shape[0], gq.shape[1], w_in.shape[0] // 4
    part_rows = QR + KR + rows + 16
    each = span + EXTRA
    buffer = lambda *shape: pltpu.VMEM(shape, bf16)
    return remote_call(
        finish_kernel,
        name_id,
        (jax.ShapeDtypeStruct((part_rows, width), bf16), jax.ShapeDtypeStruct((span, D), f32)),
        [
            buffer(8 * each, PACK),
            buffer(each, PACK),
            buffer(4, each, PACK),
            buffer(4, each, PACK),
        ]
        + [buffer(2, each // 2, PACK)] * 4
        + [
            buffer(4 * span, rows),
            buffer(4, (QR + KR) // 4, width),
            buffer(span, PACK),
            buffer(4 * span, PACK),
            buffer(rows, PACK),
            buffer(rows // 2, PACK),
        ],
        20,
        operands,
    )


def gain_grad(gain, pairs):
    return sum(jnp.sum(w.astype(f32) * grad, axis=1) for w, grad in pairs) / gain


def unpack_kernel(
    total, qup, lup, qd, ld, gain_a, gain_q, gain_l, up, lu, out, qg, lg, a_out, q_out, l_out, f_out
):
    width = total.shape[2]
    heads = width // LANES
    q_rows, l_rows = qup.shape[0], lup.shape[0]
    rows = q_rows + l_rows
    each = heads * DV
    base = D // width * each
    lane = lax.broadcasted_iota(jnp.int32, (q_rows, LANES), 1)
    own = DN + DR

    def head(number):
        seat, side = number // (2 * heads), number // heads % 2
        at = number % heads * LANES
        begin = base + seat * rows
        return total[side, begin : begin + q_rows, at : at + LANES].astype(f32)

    turn = lambda values, by: pltpu.roll(values, by % LANES, 1)
    q_sum = jnp.zeros((q_rows, 1), f32)
    for first in range(0, H, 4):
        a, b, c, d = (head(first + i) for i in range(4))
        merged = (
            jnp.where(lane < own, a, turn(b, own)),
            jnp.where(lane < 2 * own - LANES, turn(b, -32), turn(c, 2 * own - LANES)),
            jnp.where(lane < own - DN, turn(c, -DN), turn(d, own - DN)),
        )
        for i, values in enumerate(merged):
            at = first * own + i * LANES
            up[:, at : at + LANES] = values
            q_sum += jnp.sum(values * qup[:, at : at + LANES].astype(f32), axis=1, keepdims=True)
    q_out[...] = q_sum / gain_q[...].astype(f32)
    l_sum = jnp.zeros((l_rows, 1), f32)
    for seat in range(4):
        for side in range(2):
            at = (seat * 2 + side) * width
            first = base + seat * rows + q_rows
            values = total[side, first : first + l_rows, :].astype(f32)
            lu[:, at : at + width] = values
            l_sum += jnp.sum(values * lup[:, at : at + width].astype(f32), axis=1, keepdims=True)
    l_out[...] = l_sum / gain_l[...].astype(f32)
    for part in range(D // width):
        for side in range(2):
            at = part * each
            out[side * each : (side + 1) * each, part * width : (part + 1) * width] = total[
                side, at : at + each, :
            ].astype(f32)
    first = base + 4 * rows
    half = qd.shape[0] // 2
    f_out[...] = total[0, first + 2 * half : first + 2 * half + 1, : f_out.shape[1]].astype(f32)
    for side in range(2):
        mine = slice(side * half, (side + 1) * half)
        left = total[side, first : first + half, :].astype(f32)
        right = total[side, first + half : first + 2 * half, : PACK - width].astype(f32)
        qg[mine, :width] = left
        qg[mine, width:] = right[:, : QR - width]
        lg[mine, :] = right[:, QR - width : DOWN - width]
        weighted = jnp.sum(left * qd[mine, :width].astype(f32), axis=1, keepdims=True)
        weighted += jnp.sum(
            right[:, : QR - width] * qd[mine, width:].astype(f32), axis=1, keepdims=True
        )
        weighted += jnp.sum(
            right[:, QR - width : DOWN - width] * ld[mine, :].astype(f32), axis=1, keepdims=True
        )
        a_out[mine, :] = weighted / gain_a[mine, :].astype(f32)


def unpack(total, qup, lup, qd, ld, gain_a, gain_q, gain_l):
    shape = lambda *dims: jax.ShapeDtypeStruct(dims, f32)
    rows = lambda weight: weight.shape[0]
    return pl.pallas_call(
        unpack_kernel,
        out_shape=(
            shape(*qup.shape),
            shape(*lup.shape),
            shape(rows(qd), D),
            shape(*qd.shape),
            shape(*ld.shape),
            shape(rows(qd), 1),
            shape(rows(qup), 1),
            shape(rows(lup), 1),
            shape(1, rows(qd)),
        ),
        compiler_params=pltpu.CompilerParams(vmem_limit_bytes=60 * MIB),
        cost_estimate=pl.CostEstimate(flops=0, bytes_accessed=24 * MIB, transcendentals=0),
    )(total, qup, lup, qd, ld, gain_a[:, None], gain_q[:, None], gain_l[:, None])


def body(
    layer_input,
    segment_ids,
    attn_gain,
    query_down,
    query_gain,
    query_up,
    latent_down,
    latent_gain,
    latent_up,
    attn_output,
    ffn_gain,
    gate_up,
    down_proj,
    cotangent,
):
    span = layer_input.shape[1]
    length = segment_ids.shape[1]
    n_f = lax.axis_size("fsdp")
    n_c = lax.axis_size("ctx")
    n_h = n_c if H % (n_f * n_c) == 0 else 1
    square = n_f == 4 and n_c == 2 and lax.axis_size("dp") == 4
    heads = H // (n_f * n_h)
    ctx = lax.axis_index("ctx") if n_h > 1 else 0
    fsdp = lax.axis_index("fsdp")
    group = lax.axis_index(("dp", "ctx"))
    place = jnp.reshape(group, (1,)).astype(jnp.int32)
    offset = lax.axis_index(PLANE) * span

    seg = segment_ids[0]
    seg_col = seg[:, None]
    seg_row = seg[None, :]
    own_q = heads * (DN + DR)
    own_kv = heads * (DN + DV)

    def own_columns(weight, width):
        rows = weight.shape[0]
        parts = weight.reshape(rows, n_f, n_h, width)
        parts = lax.dynamic_index_in_dim(parts, ctx, 2, keepdims=False)
        parts = jnp.transpose(parts, (1, 0, 2))
        return lax.all_to_all(parts, "fsdp", 0, 0, tiled=False).reshape(rows * n_f, width)

    wo = lax.dynamic_slice_in_dim(attn_output, ctx * heads * DV, heads * DV, 0)
    wo = jnp.pad(wo.reshape(heads, DV, D), ((0, 0), (LANES - DV, 0), (0, 0)))
    wo = wo.reshape(heads * LANES, D)
    def gather_plane(shard, name_id):
        if square:
            return plane_gather(shard, name_id)
        return lax.all_gather(shard, PLANE, axis=0, tiled=True)

    def scatter_plane(part, name_id):
        if square:
            return plane_scatter(part, name_id)
        if n_h > 1:
            return lax.psum_scatter(part, PLANE, scatter_dimension=0, tiled=True)
        half = length // n_c
        part = lax.dynamic_slice_in_dim(part, lax.axis_index("ctx") * half, half, 0)
        return lax.psum_scatter(part, "fsdp", scatter_dimension=0, tiled=True)

    def gather_heads(part):
        return lax.all_gather(part, "ctx", axis=0) if n_h > 1 else part[None]

    inputs = layer_input[0].astype(f32)
    grad_out = cotangent[0].astype(f32)
    if square:
        lat, wq, wl, w_down_in, raw, normed_in, gains, cos_all, sin_all = front(
            layer_input[0],
            query_down,
            latent_down,
            (attn_gain, ffn_gain, query_gain, latent_gain),
            query_up,
            latent_up,
            seg_col,
            seg_row,
            heads,
            1,
        )
        g_attn, g_ffn, g_query, g_latent = gains[0], gains[1], gains[2, :QR], gains[3, :KR]
    else:
        gather = lambda shard: lax.all_gather(shard, "fsdp", axis=0, tiled=True)
        g_attn, g_ffn, g_query, g_latent = (
            gather(g).astype(f32) for g in (attn_gain, ffn_gain, query_gain, latent_gain)
        )
        blank = jnp.zeros((query_down.shape[0], PACK - DOWN), bf16)
        w_down_in = gather(jnp.concatenate([query_down, latent_down, blank], axis=1))
        wq = own_columns(query_up, own_q).reshape(QR, heads, DN + DR)
        wq = jnp.pad(wq, ((0, 0), (0, 0), (0, LANES - DN - DR))).reshape(QR, heads * LANES)
        wl = own_columns(latent_up, own_kv)
        starts = [jnp.sum((seg < number).astype(jnp.int32)) for number in range(4)]
        doc_start = sum(jnp.where(seg == number, starts[number], 0) for number in range(1, 4))
        cosine, sine = angles((jnp.arange(length, dtype=jnp.int32) - doc_start).astype(f32))
        ones = jnp.ones((length, DN), f32)
        rest = jnp.zeros((length, LANES - DN - DR), f32)
        cos_all = jnp.concatenate([ones, cosine, cosine, rest], axis=1)
        sin_all = jnp.concatenate([0.0 * ones, sine, sine, rest], axis=1)
        cos_own = lax.dynamic_slice_in_dim(cosine, offset, span, 0)
        sin_own = lax.dynamic_slice_in_dim(sine, offset, span, 0)
        normed_in = normalize(inputs, g_attn).astype(bf16)
        raw = dot(normed_in, w_down_in)
        query_normed = normalize(raw[:, :QR], g_query).astype(bf16)
        latent = normalize(raw[:, QR : QR + KR], g_latent).astype(bf16)
        key_rope = rotate(raw[:, QR + KR : DOWN], cos_own, sin_own).astype(bf16)
        key_rope = jnp.pad(key_rope, ((0, 0), (DN, LANES - DN - DR)))
        lat = jnp.concatenate([query_normed, latent, key_rope], axis=1)
        lat = lax.all_gather(lat, PLANE, axis=0, tiled=True)
    query_latent = raw[:, :QR]
    latent_pre = raw[:, QR : QR + KR]
    operands = (lat, wq, wl, cos_all, sin_all, seg_col, seg_row)
    if square:
        cot_z = lax.all_gather(cotangent[0], "dp", axis=0)
        q, k, kv, o, lse, cot_all = attend(*operands, cotangent[0], 4 * length, 2)
        diagonal = ((1 - ctx) * 4 + (fsdp + 2) % 4) * span
        cot_far = lax.all_gather(
            lax.dynamic_slice(cot_all, (diagonal, 0), (span, D)), "dp", axis=0
        )
    else:
        cot_all = lax.all_gather(cotangent[0], ALL, axis=0, tiled=True)
        q, k, kv, o, lse = attend(*operands)
    branch = scatter_plane(dot(o, wo).astype(bf16), 3)
    resid = inputs + RESIDUAL_SCALE * branch.astype(f32)

    ffn_in = normalize(resid, g_ffn).astype(bf16)
    own = n_f * span
    if square:
        ffn_in, cot_z = lax.optimization_barrier((ffn_in, cot_z))
        x_z = lax.all_gather(ffn_in, "dp", axis=0)
        h_all, g_all, gx, y_keep, y_send, x_all = ffn_group(
            ffn_in, cot_all, gate_up, down_proj, 4
        )
        x_far = lax.all_gather(lax.dynamic_slice(x_all, (diagonal, 0), (span, D)), "dp", axis=0)
    else:
        x_own = lax.all_gather(ffn_in, "fsdp", axis=0, tiled=True)
        h_all, g_all, y_part, gx_part = ffn_own(place, x_own, cot_all, gate_up, down_proj)
        gx = lax.psum_scatter(gx_part, "fsdp", scatter_dimension=0, tiled=True)
        y = lax.psum_scatter(y_part, "fsdp", scatter_dimension=0, tiled=True).astype(f32)
    gx = gx.astype(f32)
    grad_resid_add, ffn_gain_part = norm_back(resid, g_ffn, gx)
    grad_resid = grad_out + grad_resid_add
    gb = (RESIDUAL_SCALE * grad_resid).astype(bf16)
    if square:
        gb, cot_far = lax.optimization_barrier((gb, cot_far))
    gb = gather_plane(gb, 6)
    operands = (gb, wo, q, k, kv, o, lse, cos_all, sin_all, seg_col, seg_row)
    if square:
        bulk = (x_z, cot_z, cot_far, x_all, cot_all)
        gq, gkv, rope, out_part, x_all, cot_all = attend_back(*operands, bulk, 4 * length, 9)
        rope, out_part, x_z, x_far = lax.optimization_barrier((rope, out_part, x_z, x_far))
        width = heads * LANES
        out_part = [out_part[:, at : at + width] for at in range(0, D, width)]
        out_total = lax.psum(jnp.concatenate(out_part[:-1], axis=0), "dp")
    else:
        x_all = lax.all_gather(ffn_in, ALL, axis=0, tiled=True)
        gq, gkv, rope, out_part = attend_back(*operands)
    width = heads * LANES
    q_rows, l_rows = QR // n_f, KR // n_f
    if square:
        part, input_grad = finish(
            (
                gq,
                gkv,
                rope,
                lat,
                wq,
                wl,
                w_down_in,
                raw,
                normed_in,
                layer_input[0],
                grad_resid,
                gains,
                cos_all,
                sin_all,
                ffn_gain_part[None],
            ),
            7,
        )
    else:
        lat_part = jnp.concatenate([dot(gq, wq, NT), dot(gkv, wl, NT), rope], axis=1).astype(bf16)
        extra = jnp.pad(ffn_gain_part.astype(bf16).reshape(n_f, -1), ((0, 0), (0, PACK - D // n_f)))
        extra = jnp.broadcast_to(extra[None, :, None], (n_c, n_f, EXTRA, PACK))
        extra = extra.reshape(n_c * n_f, EXTRA, PACK)
        lat_part = jnp.concatenate([lat_part.reshape(n_c * n_f, span, PACK), extra], axis=1)
        lat_sum = scatter_plane(lat_part.reshape(-1, PACK), 7).astype(f32)
        lat_grad = lat_sum[:span]
        ffn_gain_plane = lat_sum[span, : D // n_f]
        query_pre = norm_back(query_latent, g_query, lat_grad[:, :QR])[0]
        latent_back = norm_back(latent_pre, g_latent, lat_grad[:, QR : QR + KR])[0]
        rope_back = unrotate(lat_grad[:, QR + KR + DN : QR + KR + DN + DR], cos_own, sin_own)
        raw_grad = jnp.concatenate(
            [query_pre, latent_back, rope_back, jnp.zeros((span, PACK - DOWN), f32)], axis=1
        ).astype(bf16)
        input_add = norm_back(inputs, g_attn, dot(raw_grad, w_down_in, NT))[0]
        input_grad = grad_resid + input_add

        own_rows = D // n_f
        n_all = lax.all_to_all(
            jnp.transpose(normed_in.reshape(span, n_f, own_rows), (1, 0, 2)), "fsdp", 0, 0
        ).reshape(n_f * span, own_rows)
        raw_all = lax.all_gather(raw_grad, "fsdp", axis=0, tiled=True)
        down_in_part = dot(n_all, raw_all, TN)[:, :DOWN]
        gain_column = ffn_gain_plane[:, None] / n_c
        blank = jnp.zeros((own_rows, PACK - DOWN - 1), f32)
        down_in_part = jnp.concatenate([down_in_part, gain_column, blank], axis=1).astype(bf16)
        width = heads * LANES
        out_part = [out_part[:, at : at + width] for at in range(0, D, width)]
        up_part = dot(lat[:, :QR], gq, TN).astype(bf16).reshape(n_f, -1, width)
        lup_part = dot(lat[:, QR : QR + KR], gkv, TN).astype(bf16).reshape(n_f, -1, width)
        swap = lax.all_to_all(jnp.concatenate([up_part, lup_part], axis=1), "fsdp", 0, 0)
        q_rows, l_rows = QR // n_f, KR // n_f
        pieces = [swap.reshape(-1, width)] + out_part
        part = jnp.concatenate(pieces, axis=0)

    if square:
        part, x_z, y_keep, y_send, out_total = lax.optimization_barrier(
            (part, x_z, y_keep, y_send, out_total)
        )
        total = lax.psum(jnp.concatenate([out_part[-1], part], axis=0), "dp")
        y_far = lax.ppermute(y_send, "fsdp", [(i, (i + 2) % 4) for i in range(4)])
        y = y_keep.astype(f32) + y_far.astype(f32)
        x_all, cot_all, h_all, g_all = ffn_others(
            x_z, cot_z, x_far, cot_far, x_all, cot_all, h_all, g_all, gate_up, down_proj, 10
        )
    else:
        part, x_all = lax.optimization_barrier((part, x_all))
        total = lax.psum(part, "dp")
        h_all, g_all = ffn_rest(place, x_all, cot_all, gate_up, down_proj, h_all, g_all, own)
    output = resid + RESIDUAL_SCALE * y
    if square:
        out_total, total, h_all = lax.optimization_barrier((out_total, total, h_all))
        total = jnp.concatenate([out_total, total], axis=0)
    else:
        total, h_all = lax.optimization_barrier((total, h_all))
    total = gather_heads(total)
    gate_up_grad = lax.dot_general(g_all, x_all, (((2,), (0,)), ((), ())), preferred_element_type=f32)
    down_grad = dot(h_all, cot_all) * RESIDUAL_SCALE

    if square:
        up_grad, lup_grad, out_grad, q_down_grad, l_down_grad, ga, gq, gl, gf = unpack(
            total,
            query_up,
            latent_up,
            query_down,
            latent_down,
            attn_gain,
            query_gain,
            latent_gain,
        )
        gain_grads = [ga[:, 0], gq[:, 0], gl[:, 0], gf[0]]
    else:
        down_in_sum = lax.psum(down_in_part, ("dp", "ctx")).astype(f32)
        swapped_rows = n_f * (q_rows + l_rows)
        both = total[:, :swapped_rows].reshape(n_h, n_f, q_rows + l_rows, heads, LANES)
        up_grad = jnp.transpose(both[:, :, :q_rows, :, : DN + DR], (2, 1, 0, 3, 4))
        up_grad = up_grad.reshape(q_rows, -1).astype(f32)
        lup_grad = jnp.transpose(both[:, :, q_rows:], (2, 1, 0, 3, 4))
        lup_grad = lup_grad.reshape(l_rows, -1).astype(f32)
        out_grad = total[:, swapped_rows:].reshape(n_h, D // width, heads * DV, width)
        out_grad = jnp.transpose(out_grad, (0, 2, 1, 3)).reshape(-1, D).astype(f32)
        q_down_grad = down_in_sum[:, :QR]
        l_down_grad = down_in_sum[:, QR:DOWN]
        downs = [(query_down, q_down_grad), (latent_down, l_down_grad)]
        gain_grads = [
            gain_grad(attn_gain.astype(f32), downs),
            gain_grad(query_gain.astype(f32), [(query_up, up_grad)]),
            gain_grad(latent_gain.astype(f32), [(latent_up, lup_grad)]),
            down_in_sum[:, DOWN],
        ]

    return (
        output.astype(bf16)[None],
        input_grad[None],
        gain_grads[0],
        q_down_grad,
        gain_grads[1],
        up_grad,
        l_down_grad,
        gain_grads[2],
        lup_grad,
        out_grad,
        gain_grads[3],
        gate_up_grad,
        down_grad,
    )


def solution(mesh):
    in_specs = (
        P("dp", ("ctx", "fsdp"), None),
        P("dp", None),
        P("fsdp"),
        P("fsdp", None),
        P("fsdp"),
        P("fsdp", None),
        P("fsdp", None),
        P("fsdp"),
        P("fsdp", None),
        P("fsdp", None),
        P("fsdp"),
        P(None, "fsdp", None),
        P("fsdp", None),
        P("dp", ("ctx", "fsdp"), None),
    )
    out_specs = (
        P("dp", ("ctx", "fsdp"), None),
        P("dp", ("ctx", "fsdp"), None),
        P("fsdp"),
        P("fsdp", None),
        P("fsdp"),
        P("fsdp", None),
        P("fsdp", None),
        P("fsdp"),
        P("fsdp", None),
        P("fsdp", None),
        P("fsdp"),
        P(None, "fsdp", None),
        P("fsdp", None),
    )
    return jax.shard_map(body, mesh=mesh, in_specs=in_specs, out_specs=out_specs, check_vma=False)
```

time: 4100 us -> 634 us (0.15)
  waiting for transfers between devices: 3470 us -> 0.87 us
  Pallas kernels: 0 us -> 438 us
  local copies, waits for them, and re-layouts: 187 us -> 22.7 us
  matrix products: 279 us -> 128 us
  blocking collectives: 62.8 us -> 0 us
  other arithmetic: 71.4 us -> 20.4 us
    unnamed x21 -> x7, waiting for transfers between devices: 1650 us -> 0.78 us
    psum x1 -> x2, waiting for transfers between devices: 866 us -> 0.04 us  [the longest x1 0.02 us: body(): out_total = lax.psum(jnp.concatenate(out_part[:-1], axis=0), 'dp')]
    all_gather x8 -> x5, waiting for transfers between devices: 731 us -> 0.05 us  [the longest x1 0.02 us: body(): x_z = lax.all_gather(ffn_in, 'dp', axis=0)]
    pallas_call x0 -> x9, Pallas kernels: none -> 438 us  [the longest x4 175 us: remote_call(): pl.pallas_call(kernel, out_shape=out_shape, in_specs=[pl.BlockSpec(memory...]
    reduce_scatter x4 -> x0, waiting for transfers between devices: 220 us -> none  [the longest x1 106 us: body(): lax.psum_scatter(out_full.astype(jnp.bfloat16), 'fsdp', scatter_dimension...]
    dot_general x65 -> x3, matrix products: 279 us -> 128 us  [the longest x1 79.4 us: body(): lax.dot_general(g_all, x_all, (((2,), (0,)), ((), ())), preferred_element...]
    convert_element_type x5 -> x0, local copies, waits for them, and re-layouts: 119 us -> none  [the longest x1 112 us: body(): terms.reshape(rows_own * lax.axis_size('fsdp'), 3 * D).astype(jnp.bfloat16)]
    convert_element_type x25 -> x2, other arithmetic: 49.6 us -> 2.99 us  [the longest x1 1.87 us: body(): gb = (RESIDUAL_SCALE * grad_resid).astype(bf16)]
  transfers between devices with their start and end apart: 17 -> 8, of which waited for: 16 -> 0; matrix products, arithmetic and copies ran while one was open for 9% -> 25% of each run, Pallas kernels for 0% -> 68%
where the time goes in v1:
time: 634 us; the launch traced here: 627 us
  Pallas kernels  438 us (69%)
  matrix products  128 us (20%)
  local copies, waits for them, and re-layouts  22.7 us (4%)
  other arithmetic  20.4 us (3%)
  between operations  14.7 us (2%)
    pallas_call x4, Pallas kernels, remote_call(): pl.pallas_call(kernel, out_shape=out_shape, in_specs=[pl.BlockSpec(memory...  175 us
    pallas_call x1, Pallas kernels, ffn_others(): pl.pallas_call(functools.partial(ffn_others_kernel, span), out_shape=[jax...  117 us
    dot_general x1, matrix products, body(): lax.dot_general(g_all, x_all, (((2,), (0,)), ((), ())), preferred_element...  79.4 us
    pallas_call x1, Pallas kernels, attend_back(): pl.pallas_call(functools.partial(attend_back_kernel, min(256, length), un...  53.8 us
    dot_general x2, matrix products, dot(): return lax.dot_general(left, right, dims, preferred_element_type=f32)  48.4 us
    pallas_call x1, Pallas kernels, ffn_group(): pl.pallas_call(functools.partial(ffn_group_kernel, columns), out_shape=ff...  48.4 us
    pallas_call x1, Pallas kernels, attend(): pl.pallas_call(functools.partial(attend_kernel, min(256, length), units),...  32.4 us
  transfers between devices with their start and end apart: 8, of which 0 were waited for; matrix products, arithmetic and copies ran while one was open for 25% of the time, Pallas kernels for 68%

profile of v1, /device:TPU:0, one launch (start us, length us, event | category | flops | bytes accessed | tf_op | source)
XLA Modules:
  0.0 626.8 jit_solution(9158034449931208000)
XLA Ops:
  7.2 0.0 all-gather.10.cloned.1.call-start
  7.2 0.7 all-gather.10.cloned.1.call-update
  7.9 0.0 all-gather.12.cloned.1.call-start
  8.0 2.0 copy.47.ld
  9.9 1.3 broadcast_in_dim.33.gain_a
  11.2 1.3 broadcast_in_dim.34.gain_f
  12.5 1.2 broadcast_in_dim.35.gain_q
  13.7 1.7 copy.48.seg_col
  15.4 55.2 %shard_map.246 = (bf16[1024,1152]{1,0:T(8,128)(2,1)}, bf16[768,640]{1,0:T(8,128)(2,1)}, bf16[256,640]{1,0:T(8,128)(2,1)}, bf16[2560,1152]{1,0:T(8,128)(2,1)}, f3...) custom-call(bf16[128,2560]{1,0:T(8,128)(2,1)} %bitcast.31, ...), custom_call_target="tpu_custom_call" | custom-call | tf_op jit(solution)/shard_map/pallas_call | solution.py:545
  70.6 0.0 copy-start.10
  70.6 32.4 %shard_map.247 = (bf16[1024,640]{1,0:T(8,128)(2,1)}, bf16[1024,640]{1,0:T(8,128)(2,1)}, bf16[1024,640]{1,0:T(8,128)(2,1)}, bf16[1024,640]{1,0:T(8,128)(2,1)}, f3...) custom-call(bf16[1024,1152]{1,0:T(8,128)(2,1)} %get-tuple-element.71.lat, bf16[768,640]{1,0:T(8,128)(2,1)} %get-tuple-element.72.wq, ...), custom_call_target="tpu_custom_call" | custom-call | flops 4026531840 | bytes 10485760 | tf_op jit(solution)/shard_map/pallas_call | solution.py:279
  103.1 2.0 constant_dynamic-slice_fusion.1
  105.0 0.0 all-gather.12.cloned.1.call-update
  105.0 0.5 all-gather.14.cloned.1.call-start
  105.6 0.1 constant_dynamic-slice_fusion.2
  105.7 0.3 pad.4
  106.0 1.7 copy-done.4
  107.7 6.0 convolution_convert_fusion.part
  113.7 30.3 %shard_map.248 = bf16[128,2560]{1,0:T(8,128)(2,1)} custom-call(bf16[1024,2560]{1,0:T(8,128)(2,1)} %convolution_convert_fusion.part), custom_call_target="tpu_custom_call" | custom-call | tf_op jit(solution)/shard_map/pallas_call | solution.py:545
  144.0 1.0 slice_reduce_fusion
  145.0 1.4 multiply_reduce_fusion
  146.4 1.1 multiply_convert_fusion.1.x
  147.5 0.0 all-gather.14.cloned.1.call-update
  147.6 0.0 all-gather.16.cloned.1.call-start
  147.6 48.4 %shard_map.249 = (bf16[1600,4096]{1,0:T(8,128)(2,1)}, bf16[2,1600,4096]{2,1,0:T(8,128)(2,1)}, bf16[128,2560]{1,0:T(8,128)(2,1)}, bf16[128,2560]{1,0:T(8,128)(2,1...) custom-call(bf16[128,2560]{1,0:T(8,128)(2,1)} %multiply_convert_fusion.1.x, ...), custom_call_target="tpu_custom_call" | custom-call | flops 25165824000 | bytes 24576000 | tf_op jit(solution)/shard_map/pallas_call | solution.py:1066
  196.0 2.0 constant_dynamic-slice_fusion
  198.0 0.0 all-gather.16.cloned.1.call-update
  198.0 0.0 all-reduce.4.cloned.1.call-start
  198.1 0.6 fusion.5
  198.7 0.4 copy-done.6
  199.1 1.9 multiply_convert_fusion
  201.0 30.8 %shard_map.250.gb = bf16[1024,2560]{1,0:T(8,128)(2,1)} custom-call(bf16[128,2560]{1,0:T(8,128)(2,1)} %get-tuple-element.81.x), custom_call_target="tpu_custom_call" | custom-call | tf_op jit(solution)/shard_map/pallas_call | solution.py:545
  231.8 0.0 all-gather.14.cloned.1.call-done
  231.8 53.8 %shard_map.251 = (bf16[1024,640]{1,0:T(8,128)(2,1)}, bf16[1024,640]{1,0:T(8,128)(2,1)}, f32[1024,128]{1,0:T(8,128)}, bf16[320,2560]{1,0:T(8,128)(2,1)}, bf16[409...) custom-call(bf16[1024,2560]{1,0:T(8,128)(2,1)} %shard_map.250.gb, ...), custom_call_target="tpu_custom_call", output_to_operand_aliasing={{4}: (14, {}), {5}: (15, {})} | custom-call | flops 13421772800 | bytes 15728640 | tf_op jit(solution)/shard_map/pallas_call | solution.py:394
  285.6 0.0 all-gather.16.cloned.1.call-done
  285.6 1.5 fusion.10
  287.2 0.0 copy-start.13
  287.2 1.1 pad_maximum_fusion.2
  288.3 0.0 all-reduce.4.cloned.1.call-update
  288.4 0.3 all-reduce.6.cloned.1.call-start
  288.6 0.8 broadcast_in_dim.43.gain_a
  289.4 0.7 broadcast_in_dim.44.gain_q
  290.2 0.7 copy.54.gain_l
  290.9 0.6 reshape.55.ffn_gain
  291.5 58.3 %shard_map.252 = (bf16[1680,640]{1,0:T(8,128)(2,1)}, f32[128,2560]{1,0:T(8,128)}) custom-call(bf16[1024,640]{1,0:T(8,128)(2,1)} %get-tuple-element.89.gq, bf16[1024,640]{1,0:T(8,128)(2,1)} %get-tuple-element.90.gkv, f32[1024,128]{1,0:T(8,128)} %get-tuple-element.93.rope, bf16[1024,1152]{1,0:T(8,128)(2,1)} %get-tuple-element.71.lat, ...), custom_call_target="tpu_custom_call" | custom-call | tf_op jit(solution)/shard_map/pallas_call | solution.py:545
  349.7 0.0 all-reduce.4.cloned.1.call-done
  349.8 1.3 collective-permute-start
  351.1 3.3 pad_maximum_fusion.1
  354.4 0.0 all-reduce.6.cloned.1.call-update
  354.4 0.4 all-gather.18.cloned.1.call-start
  354.9 117.3 %shard_map.253 = (bf16[4096,2560]{1,0:T(8,128)(2,1)}, bf16[4096,2560]{1,0:T(8,128)(2,1)}, bf16[1600,4096]{1,0:T(8,128)(2,1)}, bf16[2,1600,4096]{2,1,0:T(8,128)(2,1)}) custom-call(bf16[4,128,2560]{2,1,0:T(8,128)(2,1)} %bitcast.40, ...), custom_call_target="tpu_custom_call", output_to_operand_aliasing={{0}: (4, {}), {1}: (5, {}), {2}: (6, {}), {3}: (7, {})} | custom-call | flops 88080384000 | bytes 129433600 | tf_op jit(solution)/shard_map/pallas_call | solution.py:1223
  472.2 0.0 all-reduce.6.cloned.1.call-done
  472.2 3.9 pad_maximum_fusion
  476.2 0.0 all-gather.18.cloned.1.call-update
  476.2 79.4 %fusion = f32[2,1600,2560]{2,1,0:T(8,128)} fusion(bf16[2,1600,4096]{2,1,0:T(8,128)(2,1)} %get-tuple-element.125, bf16[4096,2560]{1,0:T(8,128)(2,1)} %get-tuple-element.126), kind=kOutput, calls=%fused_computation | convolution fusion | flops 67108864000 | bytes 79953920 | tf_op jit(solution)/shard_map/dot_general | solution.py:1754
  555.6 2.3 fusion.7
  558.0 42.4 %convolution_multiply_fusion = f32[1600,2560]{1,0:T(8,128)} fusion(bf16[1600,4096]{1,0:T(8,128)(2,1)} %get-tuple-element.127, bf16[4096,2560]{1,0:T(8,128)(2,1)} %get-tuple-element.128), kind=kOutput, calls=%fused_computation.2 | convolution fusion | flops 33558528000 | bytes 50462720 | tf_op jit(solution)/shard_map/dot_general | solution.py:39
  600.4 11.2 %shard_map.254 = (f32[192,3840]{1,0:T(8,128)}, f32[64,5120]{1,0:T(8,128)}, f32[640,2560]{1,0:T(8,128)}, f32[640,768]{1,0:T(8,128)}, f32[640,288]{1,0:T(8,128)}, ...) custom-call(bf16[2,2960,640]{2,1,0:T(8,128)(2,1)} %bitcast.35, ...), custom_call_target="tpu_custom_call" | custom-call | bytes 25165824 | tf_op jit(solution)/shard_map/pallas_call | solution.py:1503
  611.6 1.8 reduce.1
  613.5 1.6 reduce.2
  615.1 2.4 copy.55
  617.4 0.6 reduce.3
  618.1 0.6 reduce.4
  618.7 1.1 copy.65
  (36 shorter events, 0.1 us)
Async XLA Ops:
  7.2 140.4 %all-gather.10.cloned.1.call-start = ((), (), s32[]{:S(2)}) async-start(), calls=%async_computation | async-start | bytes 3276800 | tf_op jit(solution)/shard_map/all_gather | solution.py:1630
  7.9 193.1 %all-gather.12.cloned.1.call-start = ((), (), s32[]{:S(2)}) async-start(), calls=%async_computation.3 | async-start | bytes 3276800 | tf_op jit(solution)/shard_map/all_gather | solution.py:1633
  70.6 34.9 %copy-start.10 = (bf16[640,2560]{1,0:T(8,128)(2,1)S(1)}, bf16[640,2560]{1,0:T(8,128)(2,1)}, u32[]{:S(2)}) copy-start(bf16[640,2560]{1,0:T(8,128)(2,1)} %param.24) | copy-start | bytes 9830404
  105.0 126.8 %all-gather.14.cloned.1.call-start = ((), (), s32[]{:S(2)}) async-start(), calls=%async_computation.4 | async-start | bytes 3276800 | tf_op jit(solution)/shard_map/all_gather | solution.py:1646
  105.7 2.0 copy-start.8
  106.0 1.7 copy-start.4
  113.7 31.3 %copy-start = (bf16[1,128,2560]{2,1,0:T(8,128)(2,1)S(1)}, bf16[1,128,2560]{2,1,0:T(8,128)(2,1)}, u32[]{:S(2)}) copy-start(bf16[1,128,2560]{2,1,0:T(8,128)(2,1)} %param.15) | copy-start | bytes 1966084
  144.0 2.4 copy-start.2
  147.6 138.1 %all-gather.16.cloned.1.call-start = ((), (), s32[]{:S(2)}) async-start(), calls=%async_computation.5 | async-start | bytes 3276800 | tf_op jit(solution)/shard_map/all_gather | solution.py:1650
  196.0 2.1 copy-start.5
  198.0 1.1 copy-start.6
  198.0 151.7 %all-reduce.4.cloned.1.call-start = ((), (), s32[]{:S(2)}) async-start(), calls=%async_computation.1 | async-start | bytes 2457600 | tf_op jit(solution)/shard_map/psum | solution.py:1670
  287.2 1.5 copy-start.13
  287.2 2.3 copy-start.16
  287.2 3.0 copy-start.15
  288.4 183.9 %all-reduce.6.cloned.1.call-start = ((), (), s32[]{:S(2)}) async-start(), calls=%async_computation.2 | async-start | bytes 5120000 | tf_op jit(solution)/shard_map/psum | solution.py:1737
  349.8 205.8 %collective-permute-start = (bf16[128,2560]{1,0:T(8,128)(2,1)}, bf16[128,2560]{1,0:T(8,128)(2,1)}, u32[]{:S(2)}, u32[]{:S(2)}) collective-permute-start(bf16[128,2560]{1,0:T(8,128)(2,1)} %get-tuple-element.103), channel_id=1, source_target_pairs={{0,2},{1,3},{2,0},{3,1},{4,6},{5,7},{6,4},{7,5},{8,10},{9,11},{10,... | collective-permute-start | bytes 1966088 | tf_op jit(solution)/shard_map/ppermute | solution.py:1738
  354.4 246.0 %all-gather.18.cloned.1.call-start = ((), (), s32[]{:S(2)}) async-start(), calls=%async_computation.6 | async-start | bytes 11366400 | tf_op jit(solution)/shard_map/all_gather | solution.py:1581
  354.9 117.4 %copy-start.9 = (bf16[960,640]{1,0:T(8,128)(2,1)S(1)}, bf16[960,640]{1,0:T(8,128)(2,1)}, u32[]{:S(2)}) copy-start(bf16[960,640]{1,0:T(8,128)(2,1)} %all-reduce.4.cloned.1.call-done) | copy-start | bytes 3686404
  476.2 79.4 %copy-start.1 = (bf16[1,128,2560]{2,1,0:T(8,128)(2,1)S(1)}, bf16[1,128,2560]{2,1,0:T(8,128)(2,1)}, u32[]{:S(2)}) copy-start(bf16[1,128,2560]{2,1,0:T(8,128)(2,1)} %param.15) | copy-start | bytes 1966084
  476.2 79.4 %copy-start.3 = (bf16[128,2560]{1,0:T(8,128)(2,1)S(1)}, bf16[128,2560]{1,0:T(8,128)(2,1)}, u32[]{:S(2)}) copy-start(bf16[128,2560]{1,0:T(8,128)(2,1)} %shard_map.248) | copy-start | bytes 1966084
  476.2 79.4 %copy-start.11 = (bf16[128,2560]{1,0:T(8,128)(2,1)S(1)}, bf16[128,2560]{1,0:T(8,128)(2,1)}, u32[]{:S(2)}) copy-start(bf16[128,2560]{1,0:T(8,128)(2,1)} %get-tuple-element.102) | copy-start | bytes 1966084
  611.6 5.8 copy-start.12
  611.6 6.4 %copy-start.14 = (f32[1,640]{1,0:T(1,128)S(1)}, f32[1,640]{1,0:T(1,128)}, u32[]{:S(2)}) copy-start(f32[1,640]{1,0:T(1,128)} %get-tuple-element.124) | copy-start | bytes 7684
  611.6 7.0 %copy-start.7 = (f32[128,2560]{1,0:T(8,128)S(1)}, f32[128,2560]{1,0:T(8,128)}, u32[]{:S(2)}) copy-start(f32[128,2560]{1,0:T(8,128)} %get-tuple-element.104) | copy-start | bytes 3932164
Sparse Core Ops, SparseCore 0:
  9.6 57.4 all-gather.9
  105.2 55.1 all-gather.11
  162.5 53.5 all-gather.13
  218.1 53.5 all-gather.15
  288.5 58.0 all-reduce.3
  354.5 102.6 all-reduce.5
  476.3 95.1 all-gather.17

commit v2 on v1

--- a/solution.py
+++ b/solution.py
@@ -1252,6 +1252,63 @@
     )(x_z, cot_z, x_far, cot_far, x_all, cot_all, h_all, g_all, w_gu, w_down)
 
 
+def ffn_grads_kernel(g, h, x, cot, gu_out, down_out, h_kept, sem):
+    which, column = pl.program_id(0), pl.program_id(1)
+    load = pltpu.make_async_copy(h, h_kept, sem.at[0])
+    units = h.shape[0]
+    cut = units // 2
+
+    @pl.when((which == 0) & (column == 0))
+    def _():
+        load.start()
+
+    @pl.when((which == 2) & (column == 0))
+    def _():
+        load.wait()
+
+    @pl.when(which < 2)
+    def _():
+        for rows in (slice(0, cut), slice(cut, units)):
+            gu_out[0, rows, :] = dot(g[0, rows, :], x[...])
+
+    @pl.when(which == 2)
+    def _():
+        for rows in (slice(0, cut), slice(cut, units)):
+            down_out[rows, :] = dot(h_kept[rows, :], cot[...]) * RESIDUAL_SCALE
+
+
+def ffn_grads(g_all, h_all, x_all, cot_all):
+    units, tokens = h_all.shape
+    width = 256
+    columns = D // width
+    shape = jax.ShapeDtypeStruct
+    last = columns - 1
+    gate_up = lambda m, n: jnp.where(m < 2, n, last)
+    only_down = lambda m, n: jnp.where(m < 2, 0, n)
+    return pl.pallas_call(
+        ffn_grads_kernel,
+        grid=(3, columns),
+        in_specs=[
+            pl.BlockSpec((1, units, tokens), lambda m, n: (jnp.minimum(m, 1), 0, 0)),
+            pl.BlockSpec(memory_space=pl.ANY),
+            pl.BlockSpec((tokens, width), lambda m, n: (0, gate_up(m, n))),
+            pl.BlockSpec((tokens, width), lambda m, n: (0, only_down(m, n))),
+        ],
+        out_specs=[
+            pl.BlockSpec((1, units, width), lambda m, n: (jnp.minimum(m, 1), 0, gate_up(m, n))),
+            pl.BlockSpec((units, width), lambda m, n: (0, only_down(m, n))),
+        ],
+        out_shape=[shape((2, units, D), f32), shape((units, D), f32)],
+        scratch_shapes=[pltpu.VMEM((units, tokens), bf16), pltpu.SemaphoreType.DMA((1,))],
+        compiler_params=pltpu.CompilerParams(vmem_limit_bytes=62 * MIB),
+        cost_estimate=pl.CostEstimate(
+            flops=6 * tokens * units * D,
+            bytes_accessed=6 * units * tokens + 6 * tokens * D + 12 * units * D,
+            transcendentals=0,
+        ),
+    )(g_all, h_all, x_all, cot_all)
+
+
 def norm_back_rows(values, gain, grad):
     inverse = lax.rsqrt(jnp.mean(values * values, axis=-1, keepdims=True) + EPS)
     unit = values * inverse
@@ -1751,8 +1808,13 @@
     else:
         total, h_all = lax.optimization_barrier((total, h_all))
     total = gather_heads(total)
-    gate_up_grad = lax.dot_general(g_all, x_all, (((2,), (0,)), ((), ())), preferred_element_type=f32)
-    down_grad = dot(h_all, cot_all) * RESIDUAL_SCALE
+    if square:
+        gate_up_grad, down_grad = ffn_grads(g_all, h_all, x_all, cot_all)
+    else:
+        gate_up_grad = lax.dot_general(
+            g_all, x_all, (((2,), (0,)), ((), ())), preferred_element_type=f32
+        )
+        down_grad = dot(h_all, cot_all) * RESIDUAL_SCALE
 
     if square:
         up_grad, lup_grad, out_grad, q_down_grad, l_down_grad, ga, gq, gl, gf = unpack(

time: 634 us -> 637 us (level)
  Pallas kernels: 438 us -> 566 us
  matrix products: 128 us -> 5.95 us
    pallas_call x0 -> x1, Pallas kernels: none -> 120 us  [ffn_grads(): pl.pallas_call(ffn_grads_kernel, grid=(3, columns), in_specs=[pl.BlockSpe...]
    dot_general x1 -> x0, matrix products: 79.4 us -> none  [body(): lax.dot_general(g_all, x_all, (((2,), (0,)), ((), ())), preferred_element...]
    dot_general x2 -> x1, matrix products: 48.4 us -> 5.95 us  [dot(): return lax.dot_general(left, right, dims, preferred_element_type=f32)]
    pallas_call x1, Pallas kernels: 48.4 us -> 56.6 us  [ffn_group(): pl.pallas_call(functools.partial(ffn_group_kernel, columns), out_shape=ff...]
  transfers between devices with their start and end apart: 8 -> 8, of which waited for: 0 -> 0; matrix products, arithmetic and copies ran while one was open for 25% -> 5% of each run, Pallas kernels for 68% -> 88%
where the time goes in v2:
time: 637 us; the launch traced here: 630 us
  Pallas kernels  566 us (89%)
  local copies, waits for them, and re-layouts  20.1 us (3%)
  other arithmetic  19.3 us (3%)
  between operations  15 us (2%)
    pallas_call x4, Pallas kernels, remote_call(): pl.pallas_call(kernel, out_shape=out_shape, in_specs=[pl.BlockSpec(memory...  174 us
    pallas_call x1, Pallas kernels, ffn_grads(): pl.pallas_call(ffn_grads_kernel, grid=(3, columns), in_specs=[pl.BlockSpe...  120 us
    pallas_call x1, Pallas kernels, ffn_others(): pl.pallas_call(functools.partial(ffn_others_kernel, span), out_shape=[jax...  117 us
    pallas_call x1, Pallas kernels, ffn_group(): pl.pallas_call(functools.partial(ffn_group_kernel, columns), out_shape=ff...  56.6 us
    pallas_call x1, Pallas kernels, attend_back(): pl.pallas_call(functools.partial(attend_back_kernel, min(256, length), un...  53.8 us
    pallas_call x1, Pallas kernels, attend(): pl.pallas_call(functools.partial(attend_kernel, min(256, length), units),...  32.5 us
  transfers between devices with their start and end apart: 8, of which 0 were waited for; matrix products, arithmetic and copies ran while one was open for 5% of the time, Pallas kernels for 88%

profile of v2, /device:TPU:0, one launch (start us, length us, event | category | flops | bytes accessed | tf_op | source)
XLA Modules:
  0.0 629.8 jit_solution(8388484982444415612)
XLA Ops:
  7.2 0.0 copy-start.11
  7.2 0.0 all-gather.10.cloned.1.call-start
  7.3 0.7 all-gather.10.cloned.1.call-update
  8.0 0.0 all-gather.12.cloned.1.call-start
  8.0 2.0 copy.47.ld
  10.0 0.6 broadcast_in_dim.33.gain_a
  10.6 0.6 broadcast_in_dim.34.gain_f
  11.2 0.6 broadcast_in_dim.35.gain_q
  11.7 1.0 copy.48.seg_col
  12.8 55.2 %shard_map.246 = (bf16[1024,1152]{1,0:T(8,128)(2,1)}, bf16[768,640]{1,0:T(8,128)(2,1)}, bf16[256,640]{1,0:T(8,128)(2,1)}, bf16[2560,1152]{1,0:T(8,128)(2,1)}, f3...) custom-call(bf16[128,2560]{1,0:T(8,128)(2,1)} %bitcast.25, ...), custom_call_target="tpu_custom_call" | custom-call | tf_op jit(solution)/shard_map/pallas_call | solution.py:545
  67.9 0.0 copy-start.9
  67.9 32.5 %shard_map.247 = (bf16[1024,640]{1,0:T(8,128)(2,1)}, bf16[1024,640]{1,0:T(8,128)(2,1)}, bf16[1024,640]{1,0:T(8,128)(2,1)}, bf16[1024,640]{1,0:T(8,128)(2,1)}, f3...) custom-call(bf16[1024,1152]{1,0:T(8,128)(2,1)} %get-tuple-element.73.lat, bf16[768,640]{1,0:T(8,128)(2,1)} %get-tuple-element.74.wq, ...), custom_call_target="tpu_custom_call" | custom-call | flops 4026531840 | bytes 10485760 | tf_op jit(solution)/shard_map/pallas_call | solution.py:279
  100.4 2.0 constant_dynamic-slice_fusion.1
  102.4 0.0 all-gather.12.cloned.1.call-update
  102.4 0.3 all-gather.14.cloned.1.call-start
  102.7 0.1 constant_dynamic-slice_fusion.2
  102.9 0.3 pad.4
  103.2 1.7 copy-done.3
  104.9 6.0 convolution_convert_fusion.part
  110.8 30.3 %shard_map.248 = bf16[128,2560]{1,0:T(8,128)(2,1)} custom-call(bf16[1024,2560]{1,0:T(8,128)(2,1)} %convolution_convert_fusion.part), custom_call_target="tpu_custom_call" | custom-call | tf_op jit(solution)/shard_map/pallas_call | solution.py:545
  141.1 1.0 slice_reduce_fusion
  142.1 1.4 multiply_reduce_fusion
  143.6 1.1 multiply_convert_fusion.1.x
  144.7 0.0 all-gather.14.cloned.1.call-update
  144.7 0.0 all-gather.16.cloned.1.call-start
  144.8 56.6 %shard_map.249 = (bf16[1600,4096]{1,0:T(8,128)(2,1)}, bf16[2,1600,4096]{2,1,0:T(8,128)(2,1)}, bf16[128,2560]{1,0:T(8,128)(2,1)}, bf16[128,2560]{1,0:T(8,128)(2,1...) custom-call(bf16[128,2560]{1,0:T(8,128)(2,1)} %multiply_convert_fusion.1.x, ...), custom_call_target="tpu_custom_call" | custom-call | flops 25165824000 | bytes 24576000 | tf_op jit(solution)/shard_map/pallas_call | solution.py:1066
  201.4 2.0 constant_dynamic-slice_fusion
  203.4 0.0 all-gather.16.cloned.1.call-update
  203.4 0.0 all-reduce.4.cloned.1.call-start
  203.5 0.6 fusion.3
  204.1 0.4 copy-done.5
  204.5 1.9 multiply_convert_fusion
  206.4 30.7 %shard_map.250.gb = bf16[1024,2560]{1,0:T(8,128)(2,1)} custom-call(bf16[128,2560]{1,0:T(8,128)(2,1)} %get-tuple-element.83.x), custom_call_target="tpu_custom_call" | custom-call | tf_op jit(solution)/shard_map/pallas_call | solution.py:545
  237.1 0.0 all-gather.14.cloned.1.call-done
  237.1 53.8 %shard_map.251 = (bf16[1024,640]{1,0:T(8,128)(2,1)}, bf16[1024,640]{1,0:T(8,128)(2,1)}, f32[1024,128]{1,0:T(8,128)}, bf16[320,2560]{1,0:T(8,128)(2,1)}, bf16[409...) custom-call(bf16[1024,2560]{1,0:T(8,128)(2,1)} %shard_map.250.gb, ...), custom_call_target="tpu_custom_call", output_to_operand_aliasing={{4}: (14, {}), {5}: (15, {})} | custom-call | flops 13421772800 | bytes 15728640 | tf_op jit(solution)/shard_map/pallas_call | solution.py:394
  291.0 0.0 all-gather.16.cloned.1.call-done
  291.0 1.5 fusion.8
  292.5 1.1 pad_maximum_fusion.2
  293.7 0.0 all-reduce.4.cloned.1.call-update
  293.7 0.3 all-reduce.6.cloned.1.call-start
  293.9 0.8 broadcast_in_dim.43.gain_a
  294.8 0.7 broadcast_in_dim.44.gain_q
  295.5 0.7 copy.54.gain_l
  296.2 0.6 reshape.55.ffn_gain
  296.8 58.3 %shard_map.252 = (bf16[1680,640]{1,0:T(8,128)(2,1)}, f32[128,2560]{1,0:T(8,128)}) custom-call(bf16[1024,640]{1,0:T(8,128)(2,1)} %get-tuple-element.91.gq, bf16[1024,640]{1,0:T(8,128)(2,1)} %get-tuple-element.92.gkv, f32[1024,128]{1,0:T(8,128)} %get-tuple-element.95.rope, bf16[1024,1152]{1,0:T(8,128)(2,1)} %get-tuple-element.73.lat, ...), custom_call_target="tpu_custom_call" | custom-call | tf_op jit(solution)/shard_map/pallas_call | solution.py:545
  355.1 0.0 all-reduce.4.cloned.1.call-done
  355.1 1.3 collective-permute-start
  356.4 3.3 pad_maximum_fusion.1
  359.7 0.0 all-reduce.6.cloned.1.call-update
  359.7 0.3 all-gather.18.cloned.1.call-start
  360.0 0.0 copy-start.1
  360.1 117.5 %shard_map.253 = (bf16[4096,2560]{1,0:T(8,128)(2,1)}, bf16[4096,2560]{1,0:T(8,128)(2,1)}, bf16[1600,4096]{1,0:T(8,128)(2,1)}, bf16[2,1600,4096]{2,1,0:T(8,128)(2,1)}) custom-call(bf16[4,128,2560]{2,1,0:T(8,128)(2,1)} %bitcast.34, ...), custom_call_target="tpu_custom_call", output_to_operand_aliasing={{0}: (4, {}), {1}: (5, {}), {2}: (6, {}), {3}: (7, {})} | custom-call | flops 88080384000 | bytes 129433600 | tf_op jit(solution)/shard_map/pallas_call | solution.py:1223
  477.6 1.2 fusion.5
  478.8 3.9 pad_maximum_fusion
  482.8 0.0 all-gather.18.cloned.1.call-update
  482.8 120.3 %shard_map.255 = (f32[2,1600,2560]{2,1,0:T(8,128)}, f32[1600,2560]{1,0:T(8,128)}) custom-call(bf16[2,1600,4096]{2,1,0:T(8,128)(2,1)} %get-tuple-element.127.g, bf16[1600,4096]{1,0:T(8,128)(2,1)} %get-tuple-element.128.h, bf16[4096,2560]{1,0:T(8,128)(2,1)} %get-tuple-element.129.x, bf16[4096,2560]{1,0:T(8,128)(2,1)} %get-tuple-element.130.cot), custom_call_target="tpu_custom_call" | custom-call | flops 100663296000 | bytes 151388160 | tf_op jit(solution)/shard_map/pallas_call | solution.py:1288
  603.1 0.0 all-gather.18.cloned.1.call-done
  603.1 11.2 %shard_map.254 = (f32[192,3840]{1,0:T(8,128)}, f32[64,5120]{1,0:T(8,128)}, f32[640,2560]{1,0:T(8,128)}, f32[640,768]{1,0:T(8,128)}, f32[640,288]{1,0:T(8,128)}, ...) custom-call(bf16[2,2960,640]{2,1,0:T(8,128)(2,1)} %bitcast.29, ...), custom_call_target="tpu_custom_call" | custom-call | bytes 25165824 | tf_op jit(solution)/shard_map/pallas_call | solution.py:1560
  614.3 1.8 reduce.1
  616.2 1.6 reduce.2
  617.8 2.4 copy.55
  620.1 0.6 reduce.3
  620.8 0.6 reduce.4
  621.4 1.1 copy.65
  (37 shorter events, 0.1 us)
Async XLA Ops:
  7.2 2.8 copy-start.13
  7.2 3.4 copy-start.16
  7.2 4.0 copy-start.17
  7.2 4.5 copy-start.11
  7.2 137.5 %all-gather.10.cloned.1.call-start = ((), (), s32[]{:S(2)}) async-start(), calls=%async_computation | async-start | bytes 3276800 | tf_op jit(solution)/shard_map/all_gather | solution.py:1687
  8.0 198.4 %all-gather.12.cloned.1.call-start = ((), (), s32[]{:S(2)}) async-start(), calls=%async_computation.3 | async-start | bytes 3276800 | tf_op jit(solution)/shard_map/all_gather | solution.py:1690
  67.9 34.8 %copy-start.9 = (bf16[640,2560]{1,0:T(8,128)(2,1)S(1)}, bf16[640,2560]{1,0:T(8,128)(2,1)}, u32[]{:S(2)}) copy-start(bf16[640,2560]{1,0:T(8,128)(2,1)} %param.24) | copy-start | bytes 9830404
  102.4 134.7 %all-gather.14.cloned.1.call-start = ((), (), s32[]{:S(2)}) async-start(), calls=%async_computation.4 | async-start | bytes 3276800 | tf_op jit(solution)/shard_map/all_gather | solution.py:1703
  102.9 2.0 copy-start.7
  103.2 1.7 copy-start.3
  110.8 31.3 %copy-start = (bf16[1,128,2560]{2,1,0:T(8,128)(2,1)S(1)}, bf16[1,128,2560]{2,1,0:T(8,128)(2,1)}, u32[]{:S(2)}) copy-start(bf16[1,128,2560]{2,1,0:T(8,128)(2,1)} %param.15) | copy-start | bytes 1966084
  141.1 2.4 copy-start.2
  144.7 146.3 %all-gather.16.cloned.1.call-start = ((), (), s32[]{:S(2)}) async-start(), calls=%async_computation.5 | async-start | bytes 3276800 | tf_op jit(solution)/shard_map/all_gather | solution.py:1707
  201.4 2.1 copy-start.4
  203.4 1.1 copy-start.5
  203.4 151.7 %all-reduce.4.cloned.1.call-start = ((), (), s32[]{:S(2)}) async-start(), calls=%async_computation.1 | async-start | bytes 2457600 | tf_op jit(solution)/shard_map/psum | solution.py:1727
  293.7 1.8 copy-start.15
  293.7 185.2 %all-reduce.6.cloned.1.call-start = ((), (), s32[]{:S(2)}) async-start(), calls=%async_computation.2 | async-start | bytes 5120000 | tf_op jit(solution)/shard_map/psum | solution.py:1794
  355.1 122.5 %collective-permute-start = (bf16[128,2560]{1,0:T(8,128)(2,1)}, bf16[128,2560]{1,0:T(8,128)(2,1)S(1)}, u32[]{:S(2)}, u32[]{:S(2)}) collective-permute-start(bf16[128,2560]{1,0:T(8,128)(2,1)} %get-tuple-element.105), channel_id=1, source_target_pairs={{0,2},{1,3},{2,0},{3,1},{4,6},{5,7},{6,4},{7,5},{8,10},{9,11},{10,... | collective-permute-start | bytes 1966088 | tf_op jit(solution)/shard_map/ppermute | solution.py:1795
  359.7 243.4 %all-gather.18.cloned.1.call-start = ((), (), s32[]{:S(2)}) async-start(), calls=%async_computation.6 | async-start | bytes 11366400 | tf_op jit(solution)/shard_map/all_gather | solution.py:1638
  360.0 117.5 %copy-start.1 = (bf16[1,128,2560]{2,1,0:T(8,128)(2,1)S(1)}, bf16[1,128,2560]{2,1,0:T(8,128)(2,1)}, u32[]{:S(2)}) copy-start(bf16[1,128,2560]{2,1,0:T(8,128)(2,1)} %param.15) | copy-start | bytes 1966084
  360.1 117.5 %copy-start.10 = (bf16[128,2560]{1,0:T(8,128)(2,1)S(1)}, bf16[128,2560]{1,0:T(8,128)(2,1)}, u32[]{:S(2)}) copy-start(bf16[128,2560]{1,0:T(8,128)(2,1)} %get-tuple-element.104) | copy-start | bytes 1966084
  477.6 1.3 copy-start.8
  614.3 5.8 copy-start.12
  614.3 6.4 %copy-start.14 = (f32[1,640]{1,0:T(1,128)S(1)}, f32[1,640]{1,0:T(1,128)}, u32[]{:S(2)}) copy-start(f32[1,640]{1,0:T(1,128)} %get-tuple-element.126) | copy-start | bytes 7684
  614.3 7.0 %copy-start.6 = (f32[128,2560]{1,0:T(8,128)S(1)}, f32[128,2560]{1,0:T(8,128)}, u32[]{:S(2)}) copy-start(f32[128,2560]{1,0:T(8,128)} %get-tuple-element.106) | copy-start | bytes 3932164
Sparse Core Ops, SparseCore 0:
  9.6 57.4 all-gather.9
  102.5 55.1 all-gather.11
  159.8 53.5 all-gather.13
  215.5 53.5 all-gather.15
  293.8 58.0 all-reduce.3
  359.9 102.6 all-reduce.5
  482.9 95.1 all-gather.17

commit v3 on v2

--- a/solution.py
+++ b/solution.py
@@ -224,11 +224,11 @@
 def attend_kernel(
     block, units, lat, wq, wl, cos, sin, seg_col, seg_row, *rest
 ):
-    sources, rest = rest[:units], rest[units:]
+    sources, rest = rest[: 2 * units], rest[2 * units :]
     (q_out, k_out, kv_out, o_out, lse_out), rest = rest[:5], rest[5:]
     length = lat.shape[0]
     if units:
-        out, local, send, recv = rest
+        out, branch_out, heads_out, local, send, recv = rest
         unit = Spread(Wires(send, recv), sources[0], out, 0, local.at[0])
 
         @pl.when(pl.program_id(0) == 0)
@@ -260,13 +260,18 @@
         o_out[first:last, :] = dot(probs, both[:last]).astype(bf16)
         lse_out[0, first:last, :] = peak + jnp.log(total)
     if units:
+        here = pl.ds(pl.multiple_of(pl.program_id(0) * LANES, LANES), LANES)
+        heads_out[:, here] = o_out[...]
 
         @pl.when(pl.program_id(0) == pl.num_programs(0) - 1)
         def _():
+            for first in range(0, length, block):
+                rows = slice(first, first + block)
+                branch_out[rows, :] = dot(heads_out[rows, :], sources[1][...]).astype(bf16)
             unit.finish()
 
 
-def attend(lat, wq, wl, cos, sin, seg_col, seg_row, cot=None, tokens=0, name_id=0):
+def attend(lat, wq, wl, cos, sin, seg_col, seg_row, cot=None, wo=None, tokens=0, name_id=0):
     length = lat.shape[0]
     heads = wq.shape[1] // LANES
     whole = lambda shape: pl.BlockSpec(shape, lambda h: (0,) * len(shape))
@@ -288,14 +293,15 @@
             whole((length, 1)),
             whole((1, length)),
         ]
-        + [whole((length // 8, D))] * units,
+        + [whole((length // 8, D)), whole((heads * LANES, D))] * units,
         out_specs=[mine(length)] * 4
         + [pl.BlockSpec((1, length, 1), lambda h: (h, 0, 0))]
-        + anywhere * units,
+        + (anywhere + [whole((length, D))]) * units,
         out_shape=[wide] * 4
         + [jax.ShapeDtypeStruct((heads, length, 1), f32)]
-        + [jax.ShapeDtypeStruct((tokens, D), bf16)] * units,
+        + [jax.ShapeDtypeStruct((tokens, D), bf16), jax.ShapeDtypeStruct((length, D), bf16)] * units,
         scratch_shapes=[
+            pltpu.VMEM((length, heads * LANES), bf16),
             pltpu.SemaphoreType.DMA((1,)),
             pltpu.SemaphoreType.DMA((wires,)),
             pltpu.SemaphoreType.DMA((wires,)),
@@ -308,7 +314,7 @@
             bytes_accessed=heads * length * LANES * 16,
             transcendentals=heads * length * length,
         ),
-    )(lat, wq, wl, cos, sin, seg_col, seg_row, *([cot] if units else []))
+    )(lat, wq, wl, cos, sin, seg_col, seg_row, *([cot, wo] if units else []))
 
 
 def attend_back_kernel(
@@ -1685,7 +1691,7 @@
     operands = (lat, wq, wl, cos_all, sin_all, seg_col, seg_row)
     if square:
         cot_z = lax.all_gather(cotangent[0], "dp", axis=0)
-        q, k, kv, o, lse, cot_all = attend(*operands, cotangent[0], 4 * length, 2)
+        q, k, kv, o, lse, cot_all, branch = attend(*operands, cotangent[0], wo, 4 * length, 2)
         diagonal = ((1 - ctx) * 4 + (fsdp + 2) % 4) * span
         cot_far = lax.all_gather(
             lax.dynamic_slice(cot_all, (diagonal, 0), (span, D)), "dp", axis=0
@@ -1693,7 +1699,8 @@
     else:
         cot_all = lax.all_gather(cotangent[0], ALL, axis=0, tiled=True)
         q, k, kv, o, lse = attend(*operands)
-    branch = scatter_plane(dot(o, wo).astype(bf16), 3)
+        branch = dot(o, wo).astype(bf16)
+    branch = scatter_plane(branch, 3)
     resid = inputs + RESIDUAL_SCALE * branch.astype(f32)
 
     ffn_in = normalize(resid, g_ffn).astype(bf16)

time: 637 us -> 639 us (level)
  transfers between devices with their start and end apart: 8 -> 8, of which waited for: 0 -> 0; matrix products, arithmetic and copies ran while one was open for 5% -> 4% of each run, Pallas kernels for 88% -> 89%
where the time goes in v3:
time: 639 us; the launch traced here: 630 us
  Pallas kernels  571 us (89%)
  local copies, waits for them, and re-layouts  21.5 us (3%)
  other arithmetic  19.3 us (3%)
  between operations  14.9 us (2%)
    pallas_call x4, Pallas kernels, remote_call(): pl.pallas_call(kernel, out_shape=out_shape, in_specs=[pl.BlockSpec(memory...  174 us
    pallas_call x1, Pallas kernels, ffn_grads(): pl.pallas_call(ffn_grads_kernel, grid=(3, columns), in_specs=[pl.BlockSpe...  120 us
    pallas_call x1, Pallas kernels, ffn_others(): pl.pallas_call(functools.partial(ffn_others_kernel, span), out_shape=[jax...  118 us
    pallas_call x1, Pallas kernels, ffn_group(): pl.pallas_call(functools.partial(ffn_group_kernel, columns), out_shape=ff...  57.2 us
    pallas_call x1, Pallas kernels, attend_back(): pl.pallas_call(functools.partial(attend_back_kernel, min(256, length), un...  54.7 us
    pallas_call x1, Pallas kernels, attend(): pl.pallas_call(functools.partial(attend_kernel, min(256, length), units),...  36.4 us
  transfers between devices with their start and end apart: 8, of which 0 were waited for; matrix products, arithmetic and copies ran while one was open for 4% of the time, Pallas kernels for 89%

profile of v3, /device:TPU:0, one launch (start us, length us, event | category | flops | bytes accessed | tf_op | source)
XLA Modules:
  0.0 629.7 jit_solution(18048083468983347043)
XLA Ops:
  7.2 0.0 copy-start.8
  7.2 0.0 all-gather.10.cloned.1.call-start
  7.3 0.7 all-gather.10.cloned.1.call-update
  8.0 0.0 all-gather.12.cloned.1.call-start
  8.0 2.0 copy.47.ld
  10.0 0.6 broadcast_in_dim.33.gain_a
  10.6 0.6 broadcast_in_dim.34.gain_f
  11.2 0.6 broadcast_in_dim.35.gain_q
  11.7 1.0 copy.48.seg_col
  12.7 1.5 constant_dynamic-slice_fusion.2
  14.3 2.0 pad.4
  16.3 55.4 %shard_map.246 = (bf16[1024,1152]{1,0:T(8,128)(2,1)}, bf16[768,640]{1,0:T(8,128)(2,1)}, bf16[256,640]{1,0:T(8,128)(2,1)}, bf16[2560,1152]{1,0:T(8,128)(2,1)}, f3...) custom-call(bf16[128,2560]{1,0:T(8,128)(2,1)} %bitcast.23, ...), custom_call_target="tpu_custom_call" | custom-call | tf_op jit(solution)/shard_map/pallas_call | solution.py:551
  71.7 36.4 %shard_map.247 = (bf16[1024,640]{1,0:T(8,128)(2,1)}, bf16[1024,640]{1,0:T(8,128)(2,1)}, bf16[1024,640]{1,0:T(8,128)(2,1)}, bf16[1024,640]{1,0:T(8,128)(2,1)}, f3...) custom-call(bf16[1024,1152]{1,0:T(8,128)(2,1)} %get-tuple-element.74.lat, ...), custom_call_target="tpu_custom_call" | custom-call | flops 4026531840 | bytes 10485760 | tf_op jit(solution)/shard_map/pallas_call | solution.py:284
  108.1 2.0 constant_dynamic-slice_fusion.1
  110.1 0.0 all-gather.12.cloned.1.call-update
  110.1 0.3 all-gather.14.cloned.1.call-start
  110.4 0.0 copy-start
  110.4 30.0 %shard_map.248 = bf16[128,2560]{1,0:T(8,128)(2,1)} custom-call(bf16[1024,2560]{1,0:T(8,128)(2,1)} %get-tuple-element.79.part), custom_call_target="tpu_custom_call" | custom-call | tf_op jit(solution)/shard_map/pallas_call | solution.py:551
  140.4 1.0 slice_reduce_fusion
  141.4 1.4 multiply_reduce_fusion
  142.8 1.1 multiply_convert_fusion.1.x
  144.0 0.0 all-gather.14.cloned.1.call-update
  144.0 0.0 all-gather.16.cloned.1.call-start
  144.0 57.2 %shard_map.249 = (bf16[1600,4096]{1,0:T(8,128)(2,1)}, bf16[2,1600,4096]{2,1,0:T(8,128)(2,1)}, bf16[128,2560]{1,0:T(8,128)(2,1)}, bf16[128,2560]{1,0:T(8,128)(2,1...) custom-call(bf16[128,2560]{1,0:T(8,128)(2,1)} %multiply_convert_fusion.1.x, ...), custom_call_target="tpu_custom_call" | custom-call | flops 25165824000 | bytes 24576000 | tf_op jit(solution)/shard_map/pallas_call | solution.py:1072
  201.2 2.0 constant_dynamic-slice_fusion
  203.3 0.0 all-gather.16.cloned.1.call-update
  203.3 0.0 all-reduce.4.cloned.1.call-start
  203.3 0.6 fusion.3
  204.0 0.4 copy-done.4
  204.3 1.9 multiply_convert_fusion
  206.2 30.0 %shard_map.250.gb = bf16[1024,2560]{1,0:T(8,128)(2,1)} custom-call(bf16[128,2560]{1,0:T(8,128)(2,1)} %get-tuple-element.84.x), custom_call_target="tpu_custom_call" | custom-call | tf_op jit(solution)/shard_map/pallas_call | solution.py:551
  236.2 0.0 all-gather.14.cloned.1.call-done
  236.2 54.7 %shard_map.251 = (bf16[1024,640]{1,0:T(8,128)(2,1)}, bf16[1024,640]{1,0:T(8,128)(2,1)}, f32[1024,128]{1,0:T(8,128)}, bf16[320,2560]{1,0:T(8,128)(2,1)}, bf16[409...) custom-call(bf16[1024,2560]{1,0:T(8,128)(2,1)} %shard_map.250.gb, ...), custom_call_target="tpu_custom_call", output_to_operand_aliasing={{4}: (14, {}), {5}: (15, {})} | custom-call | flops 13421772800 | bytes 15728640 | tf_op jit(solution)/shard_map/pallas_call | solution.py:400
  290.9 0.0 all-gather.16.cloned.1.call-done
  291.0 1.5 fusion.8
  292.5 1.1 pad_maximum_fusion.2
  293.6 0.0 all-reduce.4.cloned.1.call-update
  293.7 0.3 all-reduce.6.cloned.1.call-start
  293.9 0.8 broadcast_in_dim.43.gain_a
  294.7 0.7 broadcast_in_dim.44.gain_q
  295.4 0.7 copy.54.gain_l
  296.1 0.6 reshape.55.ffn_gain
  296.8 58.3 %shard_map.252 = (bf16[1680,640]{1,0:T(8,128)(2,1)}, f32[128,2560]{1,0:T(8,128)}) custom-call(bf16[1024,640]{1,0:T(8,128)(2,1)} %get-tuple-element.93.gq, bf16[1024,640]{1,0:T(8,128)(2,1)} %get-tuple-element.94.gkv, f32[1024,128]{1,0:T(8,128)} %get-tuple-element.97.rope, bf16[1024,1152]{1,0:T(8,128)(2,1)} %get-tuple-element.74.lat, ...), custom_call_target="tpu_custom_call" | custom-call | tf_op jit(solution)/shard_map/pallas_call | solution.py:551
  355.0 0.0 all-reduce.4.cloned.1.call-done
  355.1 0.8 collective-permute-start
  355.9 3.3 pad_maximum_fusion.1
  359.2 0.0 all-reduce.6.cloned.1.call-update
  359.2 0.3 all-gather.18.cloned.1.call-start
  359.5 0.0 copy-start.1
  359.5 118.0 %shard_map.253 = (bf16[4096,2560]{1,0:T(8,128)(2,1)}, bf16[4096,2560]{1,0:T(8,128)(2,1)}, bf16[1600,4096]{1,0:T(8,128)(2,1)}, bf16[2,1600,4096]{2,1,0:T(8,128)(2,1)}) custom-call(bf16[4,128,2560]{2,1,0:T(8,128)(2,1)} %bitcast.32, ...), custom_call_target="tpu_custom_call", output_to_operand_aliasing={{0}: (4, {}), {1}: (5, {}), {2}: (6, {}), {3}: (7, {})} | custom-call | flops 88080384000 | bytes 129433600 | tf_op jit(solution)/shard_map/pallas_call | solution.py:1229
  477.5 1.2 fusion.5
  478.8 0.0 copy-done.6
  478.8 3.9 pad_maximum_fusion
  482.7 0.0 all-gather.18.cloned.1.call-update
  482.7 120.3 %shard_map.255 = (f32[2,1600,2560]{2,1,0:T(8,128)}, f32[1600,2560]{1,0:T(8,128)}) custom-call(bf16[2,1600,4096]{2,1,0:T(8,128)(2,1)} %get-tuple-element.129.g, bf16[1600,4096]{1,0:T(8,128)(2,1)} %get-tuple-element.130.h, bf16[4096,2560]{1,0:T(8,128)(2,1)} %get-tuple-element.131.x, bf16[4096,2560]{1,0:T(8,128)(2,1)} %get-tuple-element.132.cot), custom_call_target="tpu_custom_call" | custom-call | flops 100663296000 | bytes 151388160 | tf_op jit(solution)/shard_map/pallas_call | solution.py:1294
  603.1 0.0 all-gather.18.cloned.1.call-done
  603.1 11.2 %shard_map.254 = (f32[192,3840]{1,0:T(8,128)}, f32[64,5120]{1,0:T(8,128)}, f32[640,2560]{1,0:T(8,128)}, f32[640,768]{1,0:T(8,128)}, f32[640,288]{1,0:T(8,128)}, ...) custom-call(bf16[2,2960,640]{2,1,0:T(8,128)(2,1)} %bitcast.27, ...), custom_call_target="tpu_custom_call" | custom-call | bytes 25165824 | tf_op jit(solution)/shard_map/pallas_call | solution.py:1566
  614.3 0.0 copy-start.11
  614.3 1.8 reduce.1
  616.1 1.6 reduce.2
  617.7 2.4 copy.55
  620.1 0.6 reduce.3
  620.7 0.6 reduce.4
  621.3 1.1 copy.65
  (30 shorter events, 0.1 us)
Async XLA Ops:
  7.2 2.8 copy-start.10
  7.2 3.4 copy-start.13
  7.2 4.0 copy-start.14
  7.2 4.5 copy-start.8
  7.2 136.8 %all-gather.10.cloned.1.call-start = ((), (), s32[]{:S(2)}) async-start(), calls=%async_computation | async-start | bytes 3276800 | tf_op jit(solution)/shard_map/all_gather | solution.py:1693
  8.0 198.3 %all-gather.12.cloned.1.call-start = ((), (), s32[]{:S(2)}) async-start(), calls=%async_computation.3 | async-start | bytes 3276800 | tf_op jit(solution)/shard_map/all_gather | solution.py:1696
  110.1 126.1 %all-gather.14.cloned.1.call-start = ((), (), s32[]{:S(2)}) async-start(), calls=%async_computation.4 | async-start | bytes 3276800 | tf_op jit(solution)/shard_map/all_gather | solution.py:1710
  110.4 31.0 %copy-start = (bf16[1,128,2560]{2,1,0:T(8,128)(2,1)S(1)}, bf16[1,128,2560]{2,1,0:T(8,128)(2,1)}, u32[]{:S(2)}) copy-start(bf16[1,128,2560]{2,1,0:T(8,128)(2,1)} %param.15) | copy-start | bytes 1966084
  140.4 2.4 copy-start.2
  144.0 147.0 %all-gather.16.cloned.1.call-start = ((), (), s32[]{:S(2)}) async-start(), calls=%async_computation.5 | async-start | bytes 3276800 | tf_op jit(solution)/shard_map/all_gather | solution.py:1714
  201.2 2.1 copy-start.3
  203.3 1.1 copy-start.4
  203.3 151.8 %all-reduce.4.cloned.1.call-start = ((), (), s32[]{:S(2)}) async-start(), calls=%async_computation.1 | async-start | bytes 2457600 | tf_op jit(solution)/shard_map/psum | solution.py:1734
  293.6 1.8 copy-start.12
  293.7 185.1 %all-reduce.6.cloned.1.call-start = ((), (), s32[]{:S(2)}) async-start(), calls=%async_computation.2 | async-start | bytes 5120000 | tf_op jit(solution)/shard_map/psum | solution.py:1801
  355.1 122.4 %collective-permute-start = (bf16[128,2560]{1,0:T(8,128)(2,1)}, bf16[128,2560]{1,0:T(8,128)(2,1)S(1)}, u32[]{:S(2)}, u32[]{:S(2)}) collective-permute-start(bf16[128,2560]{1,0:T(8,128)(2,1)} %get-tuple-element.107), channel_id=1, source_target_pairs={{0,2},{1,3},{2,0},{3,1},{4,6},{5,7},{6,4},{7,5},{8,10},{9,11},{10,... | collective-permute-start | bytes 1966088 | tf_op jit(solution)/shard_map/ppermute | solution.py:1802
  359.2 243.9 %all-gather.18.cloned.1.call-start = ((), (), s32[]{:S(2)}) async-start(), calls=%async_computation.6 | async-start | bytes 11366400 | tf_op jit(solution)/shard_map/all_gather | solution.py:1644
  359.5 118.0 %copy-start.1 = (bf16[1,128,2560]{2,1,0:T(8,128)(2,1)S(1)}, bf16[1,128,2560]{2,1,0:T(8,128)(2,1)}, u32[]{:S(2)}) copy-start(bf16[1,128,2560]{2,1,0:T(8,128)(2,1)} %param.15) | copy-start | bytes 1966084
  359.5 118.0 %copy-start.7 = (bf16[128,2560]{1,0:T(8,128)(2,1)S(1)}, bf16[128,2560]{1,0:T(8,128)(2,1)}, u32[]{:S(2)}) copy-start(bf16[128,2560]{1,0:T(8,128)(2,1)} %get-tuple-element.106) | copy-start | bytes 1966084
  477.5 1.3 copy-start.6
  614.3 5.8 copy-start.9
  614.3 6.4 %copy-start.11 = (f32[1,640]{1,0:T(1,128)S(1)}, f32[1,640]{1,0:T(1,128)}, u32[]{:S(2)}) copy-start(f32[1,640]{1,0:T(1,128)} %get-tuple-element.128) | copy-start | bytes 7684
  614.3 7.0 %copy-start.5 = (f32[128,2560]{1,0:T(8,128)S(1)}, f32[128,2560]{1,0:T(8,128)}, u32[]{:S(2)}) copy-start(f32[128,2560]{1,0:T(8,128)} %get-tuple-element.108) | copy-start | bytes 3932164
Sparse Core Ops, SparseCore 0:
  9.6 57.4 all-gather.9
  110.2 55.2 all-gather.11
  167.7 53.5 all-gather.13
  223.3 53.5 all-gather.15
  293.8 58.0 all-reduce.3
  359.3 102.7 all-reduce.5
  482.9 95.1 all-gather.17
